TPU v7x, 32 devices: a whole 2x2x4 slice. The times are simulated.
32 devices in a mesh: leaf: 16 (over z, y, x), grp: 2 (over core).
Axes of the slice: x: 2, y: 2, z: 4, core: 2. Of those that a mesh axis runs over, the one named last changes fastest.
Arguments:
- points: bfloat16 [256, 32768], P(None, ('leaf', 'grp')), may hold values from -6 to 6
- charges: bfloat16 [64, 32768], P(None, ('leaf', 'grp')), may hold values from -6 to 6
- order: int32 [32768], P(('leaf', 'grp')), may hold values from 0 to 1023, as said below
- near_mask: int32 [32, 5], P(('leaf', 'grp')), may hold values from 0 to 1, as said below
- skeletons: int32 [32, 5, 128], P(('leaf', 'grp')), may hold values from 0 to 1023, as said below
- leaf_interp: bfloat16 [128, 32768], P(None, ('leaf', 'grp')), may hold values from -0.5 to 0.5
- transfer: bfloat16 [32, 4, 128, 128], P(('leaf', 'grp')), as said below
Outputs:
- potentials: float32 [64, 32768], P(None, ('leaf', 'grp'))
Inputs may be any that keep to these rules, and one draw needn't show every extreme that they name: `order`: within each block of 1024 consecutive entries, a permutation of 0 to 1023. `near_mask`: entry 2 of every row is 1; an entry is 0 where it points outside the leaf coordinates; the pattern is symmetric: block b marks the block k leaf coordinates away exactly when that block marks b. Level 0 holds 128 different rows of the block; level j >= 1 holds 128 different positions of 0 to 255 in the two children's skeletons; the set of a node is the same on every block of that node. `transfer`: the matrix of a node is the same on every block of that node.
All inputs are finite; a program needn't handle non-finite values.
Results may differ from a plain program's by a relative error of at most 0.0019.
Values may be sent and summed in bfloat16 or wider, within the bound.
No kernel may reach another device: no remote copies, remote signals or barrier semaphores. Data moves between devices by JAX's collectives and lax.ppermute only.
A program may use at most 64 MiB of HBM per device.

v0:
```python
import jax
import jax.numpy as jnp
from jax import lax
from jax.sharding import PartitionSpec as P

REACH = 2


HIGHEST_PRECISION = lax.Precision.HIGHEST


def passed_along(value, axis, steps):
    count = lax.axis_size(axis)
    initial, last = (max(0, -steps), min(count, count - steps))
    return lax.ppermute(value, axis, [(source, source + steps) for source in range(initial, last)])


def from_partner(block, axis, stride):
    count = lax.axis_size(axis)
    route = []
    for low in range(count):
        high = low | 1 << stride
        if high != low and high < count:
            route += [(low, high), (high, low)]
    return lax.ppermute(block, axis, route)


def pair_kernel(source, target):
    source_wide = source.astype(jnp.float32)
    target_wide = target.astype(jnp.float32)
    source_square = jnp.sum(source_wide * source_wide, axis=0)
    target_square = jnp.sum(target_wide * target_wide, axis=0)
    inner = lax.dot_general(
        source, target, (((0,), (0,)), ((), ())), preferred_element_type=jnp.float32
    )
    return jnp.exp(
        -2.0 * (source_square[:, None] + target_square[None, :] - 2.0 * inner) / source.shape[0]
    )


def apply_tile(source, source_charges, target):
    width = min(512, target.shape[1])
    outputs = []
    for column in range(0, target.shape[1], width):
        tile = pair_kernel(source, target[:, column : column + width]).astype(jnp.bfloat16)
        outputs.append(jnp.dot(source_charges, tile, preferred_element_type=jnp.float32))
    return jnp.concatenate(outputs, axis=1)


def local(points, charges, order, near_mask, skeletons, leaf_interp, transfer):
    dimension = points.shape[0]
    sides = charges.shape[0]
    leaf_rows = points.shape[1]
    ordered = jnp.take(charges, order, axis=1)
    packed = jnp.concatenate([points, ordered], axis=0)
    near_field = jnp.zeros((sides, leaf_rows), jnp.float32)
    for offset in range(-REACH, REACH + 1):
        if offset == 0:
            neighbour = packed
        else:
            neighbour = passed_along(packed, "leaf", -offset)

        def add_tile(carry, neighbour_data=neighbour):
            return carry + apply_tile(
                neighbour_data[:dimension], neighbour_data[dimension:], points
            )

        near_field = lax.cond(
            near_mask[0, offset + REACH] > 0, add_tile, lambda carry: carry, near_field
        )
    weights_now = lax.dot_general(
        ordered, leaf_interp, (((1,), (1,)), ((), ())), preferred_element_type=jnp.float32
    )
    coords = jnp.take(points, skeletons[0, 0], axis=1).astype(jnp.float32)
    levels = lax.axis_size("leaf").bit_length() - 1
    position = lax.axis_index("leaf")
    history = []
    for level in range(1, levels + 1):
        transfer_now = transfer[0, level - 1].astype(jnp.float32)
        contrib = jnp.dot(weights_now, transfer_now.T, precision=HIGHEST_PRECISION)
        bundle = jnp.concatenate([weights_now, contrib, coords], axis=0)
        partner = from_partner(bundle, "leaf", level - 1)
        partner_weights = partner[:sides]
        partner_contrib = partner[sides : 2 * sides]
        partner_coords = partner[2 * sides :]
        history.append((coords, partner_weights, partner_coords))
        upper_bit = position >> level - 1 & 1
        lower_first = jnp.concatenate([coords, partner_coords], axis=1)
        upper_first = jnp.concatenate([partner_coords, coords], axis=1)
        joined = jnp.where(upper_bit == 0, lower_first, upper_first)
        coords = jnp.take(joined, skeletons[0, level], axis=1)
        weights_now = contrib + partner_contrib
    top_bundle = jnp.concatenate([weights_now, coords], axis=0)[None]
    everyone = lax.all_gather(top_bundle.astype(jnp.bfloat16), "grp", axis=0, tiled=True).astype(
        top_bundle.dtype
    )
    other_weights = everyone[:, :sides]
    other_coords = everyone[:, sides:].astype(jnp.bfloat16)
    own_coords = coords.astype(jnp.bfloat16)
    kernels = jax.vmap(lambda source_coords: pair_kernel(source_coords, own_coords))(other_coords)
    keep = (jnp.arange(everyone.shape[0]) != lax.axis_index("grp")).astype(jnp.float32)
    potential = jnp.einsum(
        "hrk,hkm->rm", other_weights, kernels * keep[:, None, None], precision=HIGHEST_PRECISION
    )
    for level in range(levels, 0, -1):
        child_coords, sibling_weights, sibling_coords = history[level - 1]
        transfer_now = transfer[0, level - 1].astype(jnp.float32)
        sibling_kernel = pair_kernel(
            sibling_coords.astype(jnp.bfloat16), child_coords.astype(jnp.bfloat16)
        )
        potential = jnp.dot(potential, transfer_now, precision=HIGHEST_PRECISION) + jnp.dot(
            sibling_weights, sibling_kernel, precision=HIGHEST_PRECISION
        )
    far_field = jnp.dot(potential, leaf_interp.astype(jnp.float32), precision=HIGHEST_PRECISION)
    return near_field + far_field


def solution(mesh):
    in_specs = (
        P(None, ("leaf", "grp")),
        P(None, ("leaf", "grp")),
        P(("leaf", "grp")),
        P(("leaf", "grp"), None),
        P(("leaf", "grp"), None, None),
        P(None, ("leaf", "grp")),
        P(("leaf", "grp"), None, None, None),
    )
    out_specs = P(None, ("leaf", "grp"))
    return jax.shard_map(local, mesh=mesh, in_specs=in_specs, out_specs=out_specs, check_vma=False)
```

profile of v0, /device:TPU:11, one launch (start us, length us, event | category | flops | bytes accessed | tf_op | source)
XLA Modules:
  0.0 106.7 jit_solution(16123005159326091417)
XLA Ops:
  0.0 0.7 fusion.183
  0.7 0.7 compare_and_fusion
  1.4 1.1 %copy.21 = bf16[64,1024]{0,1:T(8,128)(2,1)S(1)} copy(bf16[64,1024]{1,0:T(8,128)(2,1)} %param.20) | data formatting | bytes 262144 | tf_op args[1]
  2.5 3.2 %gather_fusion = bf16[1024,64]{1,0:T(8,128)(2,1)S(1)} fusion(bf16[64,1024]{0,1:T(8,128)(2,1)S(1)} %copy.21, s32[1024]{0:T(1024)S(1)} %fusion.183), kind=kCustom, calls=%fused_computation.4 | custom fusion | bytes 266240 | tf_op jit(solution)/shard_map/jit(_take)/gather | solution.py:54
  5.7 0.2 fusion.142
  6.1 0.7 copy-done.1
  6.8 3.1 %collective-permute-start = (bf16[320,1024]{1,0:T(8,128)(2,1)S(1)}, bf16[320,1024]{1,0:T(8,128)(2,1)}, u32[]{:S(2)}, u32[]{:S(2)}) collective-permute-start(bf16[320,1024]{1,0:T(8,128)(2,1)S(1)} %pad_maximum_fusion.1), channel_id=1, source_target_pairs={{0,4},{2,6},{4,8},{6,10},{8,12},{10,14},{12,16},{14,18},{16,20},{1... | collective-permute-start | bytes 1966088 | tf_op jit(solution)/shard_map/ppermute | solution.py:15
  10.0 3.1 %collective-permute-start.1 = (bf16[320,1024]{1,0:T(8,128)(2,1)S(1)}, bf16[320,1024]{1,0:T(8,128)(2,1)}, u32[]{:S(2)}, u32[]{:S(2)}) collective-permute-start(bf16[320,1024]{1,0:T(8,128)(2,1)S(1)} %pad_maximum_fusion.1), channel_id=1, source_target_pairs={{0,2},{2,4},{4,6},{6,8},{8,10},{10,12},{12,14},{14,16},{16,18},{18... | collective-permute-start | bytes 1966088 | tf_op jit(solution)/shard_map/ppermute | solution.py:15
  13.1 2.2 %collective-permute-start.2 = (bf16[320,1024]{1,0:T(8,128)(2,1)S(1)}, bf16[320,1024]{1,0:T(8,128)(2,1)}, u32[]{:S(2)}, u32[]{:S(2)}) collective-permute-start(bf16[320,1024]{1,0:T(8,128)(2,1)S(1)} %pad_maximum_fusion.1), channel_id=1, source_target_pairs={{2,0},{4,2},{6,4},{8,6},{10,8},{12,10},{14,12},{16,14},{18,16},{20... | collective-permute-start | bytes 1966088 | tf_op jit(solution)/shard_map/ppermute | solution.py:15
  15.3 3.0 %collective-permute-start.3 = (bf16[320,1024]{1,0:T(8,128)(2,1)S(1)}, bf16[320,1024]{1,0:T(8,128)(2,1)}, u32[]{:S(2)}, u32[]{:S(2)}) collective-permute-start(bf16[320,1024]{1,0:T(8,128)(2,1)S(1)} %pad_maximum_fusion.1), channel_id=1, source_target_pairs={{4,0},{6,2},{8,4},{10,6},{12,8},{14,10},{16,12},{18,14},{20,16},{2... | collective-permute-start | bytes 1966088 | tf_op jit(solution)/shard_map/ppermute | solution.py:15
  18.3 0.2 copy.24
  18.6 0.8 gather_fusion.1
  19.6 0.4 fusion.141
  20.0 0.2 fusion.164
  20.2 1.2 %collective-permute-start.4 = (f32[384,128]{1,0:T(8,128)S(1)}, f32[384,128]{1,0:T(8,128)S(1)}, u32[]{:S(2)}, u32[]{:S(2)}) collective-permute-start(f32[384,128]{1,0:T(8,128)S(1)} %pad_maximum_fusion.2), channel_id=1, source_target_pairs={{0,2},{2,0},{4,6},{6,4},{8,10},{10,8},{12,14},{14,12},{16,18},{18,... | collective-permute-start | bytes 589832 | tf_op jit(solution)/shard_map/ppermute | solution.py:25
  21.5 0.7 fusion.191
  25.4 20.2 %collective-permute-done.4 = f32[384,128]{1,0:T(8,128)S(1)} collective-permute-done((f32[384,128]{1,0:T(8,128)S(1)}, f32[384,128]{1,0:T(8,128)S(1)}, u32[]{:S(2)}, u32[]{:S(2)}) %collective-permute-start.4) | collective-permute-done | bytes 196640 | tf_op jit(solution)/shard_map/ppermute | solution.py:25
  45.7 0.8 gather_fusion.2
  46.6 0.2 fusion.160
  46.9 2.1 %collective-permute-start.5 = (f32[384,128]{1,0:T(8,128)S(1)}, f32[384,128]{1,0:T(8,128)S(1)}, u32[]{:S(2)}, u32[]{:S(2)}) collective-permute-start(f32[384,128]{1,0:T(8,128)S(1)} %pad_maximum_fusion.3), channel_id=1, source_target_pairs={{0,4},{4,0},{2,6},{6,2},{8,12},{12,8},{10,14},{14,10},{16,20},{20,... | collective-permute-start | bytes 589832 | tf_op jit(solution)/shard_map/ppermute | solution.py:25
  49.0 0.2 fusion.130
  49.2 9.4 %collective-permute-done.5 = f32[384,128]{1,0:T(8,128)S(1)} collective-permute-done((f32[384,128]{1,0:T(8,128)S(1)}, f32[384,128]{1,0:T(8,128)S(1)}, u32[]{:S(2)}, u32[]{:S(2)}) %collective-permute-start.5) | collective-permute-done | bytes 196640 | tf_op jit(solution)/shard_map/ppermute | solution.py:25
  58.8 0.8 gather_fusion.3
  59.7 0.2 fusion.156
  60.0 0.2 fusion.133
  60.2 5.8 %collective-permute-done.6 = f32[384,128]{1,0:T(8,128)S(1)} collective-permute-done((f32[384,128]{1,0:T(8,128)S(1)}, f32[384,128]{1,0:T(8,128)S(1)}, u32[]{:S(2)}, u32[]{:S(2)}) %collective-permute-start.6) | collective-permute-done | bytes 196640 | tf_op jit(solution)/shard_map/ppermute | solution.py:25
  66.0 0.2 fusion.152
  66.4 0.8 gather_fusion.4
  67.3 0.7 pad_maximum_fusion.5
  68.0 2.3 %collective-permute-start.7 = (f32[384,128]{1,0:T(8,128)}, f32[384,128]{1,0:T(8,128)S(1)}, u32[]{:S(2)}, u32[]{:S(2)}) collective-permute-start(f32[384,128]{1,0:T(8,128)} %pad_maximum_fusion.5), channel_id=1, source_target_pairs={{0,16},{16,0},{2,18},{18,2},{4,20},{20,4},{6,22},{22,6},{8,24},{24... | collective-permute-start | bytes 589832 | tf_op jit(solution)/shard_map/ppermute | solution.py:25
  70.3 0.2 fusion.136
  70.5 6.8 %conditional.5 = (f32[64,1024]{1,0:T(8,128)S(1)}) conditional(s32[]{:T(128)} %bitcast.14, () %tuple.36, (bf16[320,1024]{1,0:T(8,128)(2,1)}, bf16[256,1024]{1,0:T(8,128)(2,1)S(1)}) %tuple.83), branch_computations={%region_0.1_spmd, %region_1.5_spmd} | conditional | flops 677967872 | bytes 3690504 | solution.py:68
  70.7 1.2 %multiply_reduce_fusion = f32[1024]{0:T(1024)S(1)} fusion(bf16[320,1024]{1,0:T(8,128)(2,1)} %get-tuple-element.52), kind=kLoop, calls=%fused_computation.20 | loop fusion | flops 785408 | bytes 528384 | tf_op jit(solution)/shard_map/cond/branch_1_fun/reduce_sum | solution.py:31
  71.8 2.0 %fusion.2 = f32[64,512]{1,0:T(8,128)S(1)} fusion(f32[512]{0:T(512)S(1)} %get-tuple-element.74, f32[1024]{0:T(1024)S(1)} %multiply_reduce_fusion, bf16[320,1024]{1,0:T(8,128)(2,1)} %get-tuple-element.52, bf16[256,1024]{1,0:T(8,128)(2,1)S(1)} %get-tuple-element.54), kind=kOutput, calls=%fused_computation.10 | convolution fusion | flops 338165760 | bytes 1054720 | tf_op jit(solution)/shard_map/cond/branch_1_fun/dot_general | solution.py:46
  73.8 2.6 %fusion.3 = f32[64,512]{1,0:T(8,128)} fusion(f32[512]{0:T(512)S(1)} %get-tuple-element.73, f32[1024]{0:T(1024)S(1)} %multiply_reduce_fusion, bf16[320,1024]{1,0:T(8,128)(2,1)} %get-tuple-element.52, bf16[256,1024]{1,0:T(8,128)(2,1)S(1)} %get-tuple-element.54), kind=kOutput, calls=%fused_computation.11 | convolution fusion | flops 338165760 | bytes 1054720 | tf_op jit(solution)/shard_map/cond/branch_1_fun/dot_general | solution.py:46
  76.4 0.9 pad_maximum_fusion
  77.4 3.6 %conditional.7 = (f32[64,1024]{1,0:T(8,128)S(1)}) conditional(s32[]{:T(128)} %bitcast.12, f32[64,1024]{1,0:T(8,128)S(1)} %get-tuple-element.122, (bf16[256,1024]{1,0:T(8,128)(2,1)S(1)}, bf16[64,1024]{0,1:T(8,128)(2,1)S(1)}, f32[64,1024]{1,0:T(8,128)S(1)}) %tuple.85), branch_computations={%region_10.11_spmd, %region_11.15_spmd} | conditional | flops 678033408 | bytes 4214792 | solution.py:68
  77.7 0.9 fusion.54
  78.5 1.5 %fusion.55 = f32[64,512]{1,0:T(8,128)} fusion(bf16[64,1024]{0,1:T(8,128)(2,1)S(1)} %get-tuple-element.71, bf16[256,1024]{1,0:T(8,128)(2,1)S(1)} %get-tuple-element.59, f32[512]{0:T(512)S(1)} %get-tuple-element.77, f32[1024]{0:T(1024)S(1)} %multiply_reduce_fusion.6), kind=kOutput, calls=%fused_computation.67 | convolution fusion | flops 338165760 | bytes 1185792 | tf_op jit(solution)/shard_map/cond/branch_1_fun/dot_general | solution.py:46
  80.1 1.0 maximum_add_fusion.1
  81.0 5.3 %conditional.8 = (f32[64,1024]{1,0:T(8,128)S(1)}) conditional(s32[]{:T(128)} %bitcast.11, f32[64,1024]{1,0:T(8,128)S(1)} %get-tuple-element.123, (bf16[320,1024]{1,0:T(8,128)(2,1)}, bf16[256,1024]{1,0:T(8,128)(2,1)S(1)}, f32[64,1024]{1,0:T(8,128)S(1)}) %tuple.86), branch_computations={%region_15.16_spmd, %region_16.20_spmd} | conditional | flops 678033408 | bytes 3952648 | solution.py:68
  81.2 1.2 %multiply_reduce_fusion.9 = f32[1024]{0:T(1024)S(1)} fusion(bf16[320,1024]{1,0:T(8,128)(2,1)} %get-tuple-element.62), kind=kLoop, calls=%fused_computation.100 | loop fusion | flops 785408 | bytes 528384 | tf_op jit(solution)/shard_map/cond/branch_1_fun/reduce_sum | solution.py:31
  82.4 2.0 %fusion.74 = f32[64,512]{1,0:T(8,128)S(1)} fusion(f32[512]{0:T(512)S(1)} %get-tuple-element.80, f32[1024]{0:T(1024)S(1)} %multiply_reduce_fusion.9, bf16[320,1024]{1,0:T(8,128)(2,1)} %get-tuple-element.62, bf16[256,1024]{1,0:T(8,128)(2,1)S(1)} %get-tuple-element.63), kind=kOutput, calls=%fused_computation.90 | convolution fusion | flops 338165760 | bytes 1054720 | tf_op jit(solution)/shard_map/cond/branch_1_fun/dot_general | solution.py:46
  84.3 2.0 %fusion.75 = f32[64,512]{1,0:T(8,128)S(1)} fusion(f32[512]{0:T(512)S(1)} %get-tuple-element.79, f32[1024]{0:T(1024)S(1)} %multiply_reduce_fusion.9, bf16[320,1024]{1,0:T(8,128)(2,1)} %get-tuple-element.62, bf16[256,1024]{1,0:T(8,128)(2,1)S(1)} %get-tuple-element.63), kind=kOutput, calls=%fused_computation.91 | convolution fusion | flops 338165760 | bytes 1054720 | tf_op jit(solution)/shard_map/cond/branch_1_fun/dot_general | solution.py:46
  86.4 5.5 %conditional.9 = (f32[64,1024]{1,0:T(8,128)S(1)}) conditional(s32[]{:T(128)} %bitcast.10, f32[64,1024]{1,0:T(8,128)S(1)} %get-tuple-element.124, (bf16[320,1024]{1,0:T(8,128)(2,1)}, bf16[256,1024]{1,0:T(8,128)(2,1)S(1)}, f32[64,1024]{1,0:T(8,128)S(1)}) %tuple.87), branch_computations={%region_20.21_spmd, %region_21.25_spmd} | conditional | flops 678033408 | bytes 3952648 | solution.py:68
  86.7 1.2 %multiply_reduce_fusion.12 = f32[1024]{0:T(1024)S(1)} fusion(bf16[320,1024]{1,0:T(8,128)(2,1)} %get-tuple-element.65), kind=kLoop, calls=%fused_computation.128 | loop fusion | flops 785408 | bytes 528384 | tf_op jit(solution)/shard_map/cond/branch_1_fun/reduce_sum | solution.py:31
  87.9 2.0 %fusion.100 = f32[64,512]{1,0:T(8,128)S(1)} fusion(f32[512]{0:T(512)S(1)} %get-tuple-element.82, f32[1024]{0:T(1024)S(1)} %multiply_reduce_fusion.12, bf16[320,1024]{1,0:T(8,128)(2,1)} %get-tuple-element.65, bf16[256,1024]{1,0:T(8,128)(2,1)S(1)} %get-tuple-element.66), kind=kOutput, calls=%fused_computation.118 | convolution fusion | flops 338165760 | bytes 1054720 | tf_op jit(solution)/shard_map/cond/branch_1_fun/dot_general | solution.py:46
  89.9 2.0 %fusion.101 = f32[64,512]{1,0:T(8,128)S(1)} fusion(f32[512]{0:T(512)S(1)} %get-tuple-element.81, f32[1024]{0:T(1024)S(1)} %multiply_reduce_fusion.12, bf16[320,1024]{1,0:T(8,128)(2,1)} %get-tuple-element.65, bf16[256,1024]{1,0:T(8,128)(2,1)S(1)} %get-tuple-element.66), kind=kOutput, calls=%fused_computation.119 | convolution fusion | flops 338165760 | bytes 1054720 | tf_op jit(solution)/shard_map/cond/branch_1_fun/dot_general | solution.py:46
  92.2 0.8 gather_fusion.5
  93.1 0.2 multiply_reduce_fusion.24
  93.5 10.1 %all_gather.3 = bf16[2,320,128]{2,1,0:T(8,128)(2,1)S(1)} all-gather(bf16[1,320,128]{2,1,0:T(8,128)(2,1)S(1)} %copy.34), channel_id=1, replica_groups=mesh['leaf'=16,'grp'=2] {'grp'}, dimensions={0}, use_global_device_ids=true | all-gather | bytes 245760 | tf_op jit(solution)/shard_map/all_gather | solution.py:94
  103.6 0.2 fusion.127
  103.9 0.2 convolution_bitcast_fusion
  104.0 0.2 fusion.150
  104.3 0.2 fusion.139
  104.5 0.2 convolution_add_fusion.3
  104.7 0.2 fusion.154
  104.8 0.2 convolution_add_fusion.2
  105.0 0.2 fusion.158
  105.2 0.2 convolution_add_fusion.1
  105.4 0.2 fusion.162
  105.6 0.2 convolution_add_fusion
  105.7 0.3 fusion.192
  106.0 0.7 add.288
  (64 shorter events, 2.9 us)
Async XLA Ops:
  0.0 19.6 %copy-start = (bf16[128,1024]{1,0:T(8,128)(2,1)S(1)}, bf16[128,1024]{1,0:T(8,128)(2,1)}, u32[]{:S(2)}) copy-start(bf16[128,1024]{1,0:T(8,128)(2,1)} %param.24) | copy-start | bytes 786436
  5.7 1.0 copy-start.1
  6.8 11.7 %copy-start.4 = (s32[1,5,128]{2,0,1:T(1,128)S(1)}, s32[1,5,128]{2,0,1:T(1,128)}, u32[]{:S(2)}) copy-start(s32[1,5,128]{2,0,1:T(1,128)} %param.23) | copy-start | bytes 7684
  6.8 63.7 %collective-permute-start = (bf16[320,1024]{1,0:T(8,128)(2,1)S(1)}, bf16[320,1024]{1,0:T(8,128)(2,1)}, u32[]{:S(2)}, u32[]{:S(2)}) collective-permute-start(bf16[320,1024]{1,0:T(8,128)(2,1)S(1)} %pad_maximum_fusion.1), channel_id=1, source_target_pairs={{0,4},{2,6},{4,8},{6,10},{8,12},{10,14},{12,16},{14,18},{16,20},{1... | collective-permute-start | bytes 1966088 | tf_op jit(solution)/shard_map/ppermute | solution.py:15
  10.0 67.4 %collective-permute-start.1 = (bf16[320,1024]{1,0:T(8,128)(2,1)S(1)}, bf16[320,1024]{1,0:T(8,128)(2,1)}, u32[]{:S(2)}, u32[]{:S(2)}) collective-permute-start(bf16[320,1024]{1,0:T(8,128)(2,1)S(1)} %pad_maximum_fusion.1), channel_id=1, source_target_pairs={{0,2},{2,4},{4,6},{6,8},{8,10},{10,12},{12,14},{14,16},{16,18},{18... | collective-permute-start | bytes 1966088 | tf_op jit(solution)/shard_map/ppermute | solution.py:15
  13.1 67.9 %collective-permute-start.2 = (bf16[320,1024]{1,0:T(8,128)(2,1)S(1)}, bf16[320,1024]{1,0:T(8,128)(2,1)}, u32[]{:S(2)}, u32[]{:S(2)}) collective-permute-start(bf16[320,1024]{1,0:T(8,128)(2,1)S(1)} %pad_maximum_fusion.1), channel_id=1, source_target_pairs={{2,0},{4,2},{6,4},{8,6},{10,8},{12,10},{14,12},{16,14},{18,16},{20... | collective-permute-start | bytes 1966088 | tf_op jit(solution)/shard_map/ppermute | solution.py:15
  15.3 71.1 %collective-permute-start.3 = (bf16[320,1024]{1,0:T(8,128)(2,1)S(1)}, bf16[320,1024]{1,0:T(8,128)(2,1)}, u32[]{:S(2)}, u32[]{:S(2)}) collective-permute-start(bf16[320,1024]{1,0:T(8,128)(2,1)S(1)} %pad_maximum_fusion.1), channel_id=1, source_target_pairs={{4,0},{6,2},{8,4},{10,6},{12,8},{14,10},{16,12},{18,14},{20,16},{2... | collective-permute-start | bytes 1966088 | tf_op jit(solution)/shard_map/ppermute | solution.py:15
  18.6 1.4 %copy-start.2 = (bf16[1,4,128,128]{3,2,1,0:T(8,128)(2,1)S(1)}, bf16[1,4,128,128]{3,2,1,0:T(8,128)(2,1)}, u32[]{:S(2)}) copy-start(bf16[1,4,128,128]{3,2,1,0:T(8,128)(2,1)} %param.25) | copy-start | bytes 393220
  19.6 1.9 %copy-start.3 = (s32[1,5]{1,0:T(1,128)S(1)}, s32[1,5]{1,0:T(1,128)}, u32[]{:S(2)}) copy-start(s32[1,5]{1,0:T(1,128)} %param.22) | copy-start | bytes 64
  20.2 25.3 %collective-permute-start.4 = (f32[384,128]{1,0:T(8,128)S(1)}, f32[384,128]{1,0:T(8,128)S(1)}, u32[]{:S(2)}, u32[]{:S(2)}) collective-permute-start(f32[384,128]{1,0:T(8,128)S(1)} %pad_maximum_fusion.2), channel_id=1, source_target_pairs={{0,2},{2,0},{4,6},{6,4},{8,10},{10,8},{12,14},{14,12},{16,18},{18,... | collective-permute-start | bytes 589832 | tf_op jit(solution)/shard_map/ppermute | solution.py:25
  46.9 11.7 %collective-permute-start.5 = (f32[384,128]{1,0:T(8,128)S(1)}, f32[384,128]{1,0:T(8,128)S(1)}, u32[]{:S(2)}, u32[]{:S(2)}) collective-permute-start(f32[384,128]{1,0:T(8,128)S(1)} %pad_maximum_fusion.3), channel_id=1, source_target_pairs={{0,4},{4,0},{2,6},{6,2},{8,12},{12,8},{10,14},{14,10},{16,20},{20,... | collective-permute-start | bytes 589832 | tf_op jit(solution)/shard_map/ppermute | solution.py:25
  59.9 6.0 %collective-permute-start.6 = (f32[384,128]{1,0:T(8,128)S(1)}, f32[384,128]{1,0:T(8,128)S(1)}, u32[]{:S(2)}, u32[]{:S(2)}) collective-permute-start(f32[384,128]{1,0:T(8,128)S(1)} %pad_maximum_fusion.4), channel_id=1, source_target_pairs={{0,8},{8,0},{2,10},{10,2},{4,12},{12,4},{6,14},{14,6},{16,24},{24,... | collective-permute-start | bytes 589832 | tf_op jit(solution)/shard_map/ppermute | solution.py:25
  68.0 23.9 %collective-permute-start.7 = (f32[384,128]{1,0:T(8,128)}, f32[384,128]{1,0:T(8,128)S(1)}, u32[]{:S(2)}, u32[]{:S(2)}) collective-permute-start(f32[384,128]{1,0:T(8,128)} %pad_maximum_fusion.5), channel_id=1, source_target_pairs={{0,16},{16,0},{2,18},{18,2},{4,20},{20,4},{6,22},{22,6},{8,24},{24... | collective-permute-start | bytes 589832 | tf_op jit(solution)/shard_map/ppermute | solution.py:25
where the time goes:
time: 105 us; the launch traced here: 107 us
  waiting for transfers between devices  35.3 us (34%)
  matrix products  18.9 us (18%)
  starting transfers between devices  17.2 us (16%)
  local copies, waits for them, and re-layouts  11 us (10%)
  other arithmetic  10.2 us (10%)
  blocking collectives  10.1 us (10%)
  between operations  3.72 us (4%)
    ppermute x4, waiting for transfers between devices, from_partner(): return lax.ppermute(block, axis, route)  35.3 us
    dot_general x8, matrix products, apply_tile(): jnp.dot(source_charges, tile, preferred_element_type=jnp.float32)  14.9 us
    ppermute x4, starting transfers between devices, passed_along(): lax.ppermute(value, axis, [(source, source + steps) for source in range(i...  11.5 us
    all_gather x1, blocking collectives, local(): lax.all_gather(top_bundle.astype(jnp.bfloat16), 'grp', axis=0, tiled=True)  10.1 us
    ppermute x4, starting transfers between devices, from_partner(): return lax.ppermute(block, axis, route)  5.69 us
    reduce_sum x9, other arithmetic, pair_kernel(): source_square = jnp.sum(source_wide * source_wide, axis=0)  3.88 us
    gather x7, local copies, waits for them, and re-layouts, local(): coords = jnp.take(joined, skeletons[0, level], axis=1)  3.38 us
    gather x1, local copies, waits for them, and re-layouts, local(): ordered = jnp.take(charges, order, axis=1)  3.21 us
  transfers between devices with their start and end apart: 8, of which 3 were waited for; matrix products, arithmetic and copies ran while one was open for 27% of the time, Pallas kernels for 0%

commit v1 on v0

v1 whole, which is shorter than its diff:
```python
import functools

import jax
import jax.numpy as jnp
from jax import lax
from jax.experimental import pallas as pl
from jax.experimental.pallas import tpu as pltpu
from jax.sharding import PartitionSpec as P

REACH = 2
PIECES = 2
BF16 = jnp.bfloat16
F32 = jnp.float32
LOG2E = 1.4426950408889634
HIGHEST = lax.Precision.HIGHEST
PAD = 16
VMEM_LIMIT = 40 * 1024 * 1024

NN = ((1,), (0,))
NT = ((1,), (1,))
TN = ((0,), (0,))


def dot(left, right, contract=NN, precision=None):
    return lax.dot_general(
        left, right, (contract, ((), ())), preferred_element_type=F32, precision=precision
    )


def halves(value):
    high = value.astype(BF16)
    return high, (value - high.astype(F32)).astype(BF16)


def row_norms(points):
    wide = points.astype(F32)
    return jnp.sum(wide * wide, axis=0, keepdims=True)


def column_norms(points):
    wide = points.astype(F32)
    high, low = halves(wide * wide)
    ones = jnp.ones((points.shape[0], 128), BF16)
    return dot(high, ones, TN) + dot(low, ones, TN)


def one_hot(index, rows, first):
    place = lax.broadcasted_iota(jnp.int32, (rows, index.shape[1]), 0) + first
    return jnp.where(place == index, 1.0, 0.0).astype(BF16)


def small_kernel(source, target):
    scale = 2.0 * LOG2E / source.shape[0]
    inner = dot(source, target, TN)
    squares = column_norms(source)[:, : target.shape[1]] + row_norms(target)
    return jnp.exp2(scale * (2.0 * inner - squares))


def pick(first, second, index, bit):
    count = first.shape[1]
    table = jnp.concatenate(
        [one_hot(index, count, count * bit), one_hot(index, count, count * (1 - bit))], axis=0
    )
    return dot(jnp.concatenate([first, second], axis=1), table).astype(BF16)


def write_messages(weights, coords, transfers, index, near_ref, far_ref, sum_ref):
    dimension, sides = coords.shape[0], weights.shape[0]
    once = dot(weights, transfers[0].astype(F32), NT, HIGHEST)
    near_ref[:dimension] = coords
    near_ref[dimension : dimension + sides] = weights.astype(BF16)
    if len(transfers) == 1:
        near_ref[dimension + sides :] = once.astype(BF16)
        sum_ref[...] = once
        return
    twice = dot(once, transfers[1].astype(F32), NT, HIGHEST)
    near_ref[dimension + sides :] = twice.astype(BF16)
    far_ref[:dimension] = coords
    far_ref[dimension : dimension + sides] = once.astype(BF16)
    far_ref[dimension + sides : dimension + 2 * sides] = twice.astype(BF16)
    far_ref[dimension + 2 * sides :] = jnp.broadcast_to(
        index.astype(F32), (PAD, index.shape[1])
    ).astype(BF16)
    sum_ref[...] = twice


def start_kernel(bits, points, charges, order, skeletons, interp, transfer, *outs):
    pieces, (ordered_ref, coords_ref), messages = outs[:PIECES], outs[PIECES : PIECES + 2], outs[PIECES + 2 :]
    dimension, rows = points.shape
    sides = charges.shape[0]
    coords = dot(points[...], one_hot(skeletons[0:1, :], rows, 0)).astype(BF16)
    coords_ref[...] = coords
    width = rows // 4
    for column in range(0, rows, width):
        table = one_hot(order[:, column : column + width], rows, 0)
        ordered_ref[:, column : column + width] = dot(charges[...], table).astype(BF16)
    weights = dot(ordered_ref[...], interp[...], NT)
    far = messages[1] if bits == 2 else None
    write_messages(
        weights,
        coords,
        [transfer[level] for level in range(bits)],
        skeletons[1:2, :],
        messages[0],
        far,
        messages[-1],
    )
    size = rows // PIECES
    for piece in range(PIECES):
        pieces[piece][:dimension] = points[:, piece * size : (piece + 1) * size]
        pieces[piece][dimension:] = ordered_ref[:, piece * size : (piece + 1) * size]


def round_kernel(level, bits, later, skeletons, transfer, coords, total, *refs):
    position = lax.axis_index("leaf")
    dimension, count = coords.shape
    sides = total.shape[0]
    low = (position >> level) & 1
    if bits == 2:
        first, second, third = (ref[...] for ref in refs[:3])
        coords_up_ref, sibling_coords_ref, sibling_weights_ref = refs[3:6]
        outs = refs[6:]
        high = (position >> (level + 1)) & 1
        middle = pick(coords[...], first[:dimension], skeletons[level + 1 : level + 2, :], low)
        index = second[dimension + 2 * sides : dimension + 2 * sides + 1].astype(F32).astype(jnp.int32)
        sibling = pick(second[:dimension], third[:dimension], index, low)
        coords_up_ref[...] = middle
        sibling_coords_ref[...] = sibling
        span = slice(dimension, dimension + sides)
        sibling_weights_ref[...] = second[span].astype(F32) + third[span].astype(F32)
        top = pick(middle, sibling, skeletons[level + 2 : level + 3, :], high)
        span = slice(dimension + sides, dimension + 2 * sides)
        weights = (
            (total[...] + first[span].astype(F32))
            + (second[span].astype(F32) + third[span].astype(F32))
        )
    else:
        first = refs[0][...]
        outs = refs[1:]
        top = pick(coords[...], first[:dimension], skeletons[level + 1 : level + 2, :], low)
        weights = total[...] + first[dimension + sides :].astype(F32)
    level += bits
    if later == 0:
        outs[0][:dimension] = top
        outs[0][dimension:] = weights.astype(BF16)
        return
    outs[0][...] = top
    write_messages(
        weights,
        top,
        [transfer[level + step] for step in range(later)],
        skeletons[level + 1 : level + 2, :],
        outs[1],
        outs[2] if later == 2 else None,
        outs[-1],
    )


def sibling_kernel(bits, sides, coords, first, *refs):
    dimension = coords.shape[0]
    weights = first[dimension : dimension + sides].astype(F32)
    refs[-bits][...] = dot(weights, small_kernel(first[:dimension], coords[...]), NN, HIGHEST)
    if bits == 2:
        coords_up, sibling_coords, sibling_weights = refs[:3]
        refs[-1][...] = dot(
            sibling_weights[...], small_kernel(sibling_coords[...], coords_up[...]), NN, HIGHEST
        )


def self_kernel(points, ordered, transposed_ref, norms_ref, near_ref):
    dimension, rows = points.shape
    scale = 2.0 * LOG2E / dimension
    transposed_ref[...] = jnp.transpose(points[...].astype(F32)).astype(BF16)
    norms_ref[...] = column_norms(points[...]) * scale
    source_norms = row_norms(points[...]) * scale
    height = min(256, rows)
    for row in range(0, rows, height):
        band = slice(row, row + height)
        inner = dot(transposed_ref[band], points[...])
        squares = jnp.tile(norms_ref[band], (1, rows // 128)) + source_norms
        tile = jnp.exp2((2.0 * scale) * inner - squares).astype(BF16)
        near_ref[:, band] = dot(ordered[...], tile, NT)


def near_kernel(column, mask, piece, transposed, norms, ordered, total, near_ref, back_ref):
    rows, dimension = transposed.shape
    width = piece.shape[1]
    scale = 2.0 * LOG2E / dimension

    @pl.when(mask[0, column] > 0)
    def _():
        source_norms = row_norms(piece[:dimension]) * scale
        height = min(256, rows)
        back = None
        for row in range(0, rows, height):
            band = slice(row, row + height)
            inner = dot(transposed[band], piece[:dimension])
            squares = jnp.tile(norms[band], (1, width // 128)) + source_norms
            tile = jnp.exp2((2.0 * scale) * inner - squares).astype(BF16)
            near_ref[:, band] = total[:, band] + dot(piece[dimension:], tile, NT)
            part = dot(ordered[:, band], tile)
            back = part if back is None else back + part
        back_ref[...] = back.astype(BF16)

    @pl.when(mask[0, column] <= 0)
    def _():
        near_ref[...] = total[...]
        back_ref[...] = jnp.zeros_like(back_ref)


def final_kernel(levels, others, near, own_top, transfer, interp, *refs):
    tops, terms, returns, out_ref = (
        refs[:others],
        refs[others : others + levels],
        refs[others + levels : -1],
        refs[-1],
    )
    dimension = own_top.shape[0] - near.shape[0]
    potential = None
    for top in tops:
        part = dot(
            top[dimension:].astype(F32),
            small_kernel(top[:dimension], own_top[:dimension]),
            NN,
            HIGHEST,
        )
        potential = part if potential is None else potential + part
    for level in range(levels, 0, -1):
        term = terms[level - 1][...]
        if potential is not None:
            term = term + dot(potential, transfer[level - 1].astype(F32), NN, HIGHEST)
        potential = term
    high, low = halves(potential)
    total = near[...] + (dot(high, interp[...]) + dot(low, interp[...]))
    size = near.shape[1] // PIECES
    for piece in range(PIECES):
        span = slice(piece * size, (piece + 1) * size)
        part = total[:, span]
        for back in returns[piece::PIECES]:
            part = part + back[...].astype(F32)
        out_ref[:, span] = part


def call(kernel, outs, args, scalars=0, flops=0, exps=0, name=None):
    vmem = pl.BlockSpec(memory_space=pltpu.VMEM)
    smem = pl.BlockSpec(memory_space=pltpu.SMEM)
    specs = [smem] * scalars + [vmem] * (len(args) - scalars)
    moved = sum(a.size * a.dtype.itemsize for a in list(args) + list(outs))
    return pl.pallas_call(
        kernel,
        out_shape=outs,
        in_specs=specs,
        out_specs=[vmem] * len(outs),
        compiler_params=pltpu.CompilerParams(vmem_limit_bytes=VMEM_LIMIT),
        cost_estimate=pl.CostEstimate(flops=flops, bytes_accessed=moved, transcendentals=exps),
        name=name,
    )(*args)


def swapped(value, axis, flip):
    count = lax.axis_size(axis)
    return lax.ppermute(value, axis, [(place, place ^ flip) for place in range(count)])


def shape(dims, dtype):
    return jax.ShapeDtypeStruct(dims, dtype)


def local(points, charges, order, near_mask, skeletons, leaf_interp, transfer):
    dimension, rows = points.shape
    sides, count = charges.shape[0], leaf_interp.shape[0]
    leaves, groups = lax.axis_size("leaf"), lax.axis_size("grp")
    levels = leaves.bit_length() - 1
    skeletons, transfer = skeletons[0], transfer[0]
    size = rows // PIECES
    rounds = []
    level = 0
    while level < levels:
        rounds.append((level, min(2, levels - level)))
        level += rounds[-1][1]

    def message_shapes(bits):
        near = shape((dimension + 2 * sides, count), BF16)
        far = shape((dimension + 2 * sides + PAD, count), BF16)
        return [near] + [far] * (bits - 1) + [shape((sides, count), F32)]

    bits = rounds[0][1]
    *pieces_and, = call(
        functools.partial(start_kernel, bits),
        [shape((dimension + sides, size), BF16)] * PIECES
        + [shape((sides, rows), BF16), shape((dimension, count), BF16)]
        + message_shapes(bits),
        [points, charges, order.reshape(1, rows), skeletons, leaf_interp, transfer],
        flops=2 * sides * rows * rows,
        name="start",
    )
    pieces = pieces_and[:PIECES]
    ordered, coords = pieces_and[PIECES : PIECES + 2]
    messages, total = pieces_and[PIECES + 2 : -1], pieces_and[-1]

    def arrived(step):
        return [(place, place + step) for place in range(leaves - step)]

    two = [lax.ppermute(piece, "leaf", arrived(2)) for piece in pieces]
    one = []
    for piece in range(PIECES):
        if 2 * piece < PIECES and leaves > 2:
            even = lax.ppermute(pieces[piece], "leaf", arrived(1)[::2])
            odd = lax.ppermute(
                two[piece], "leaf", [(place + 1, place) for place in range(2, leaves, 2)]
            )
            keep = lax.axis_index("leaf") % 2 == 1
            one.append(jnp.where(keep, even, odd))
        else:
            one.append(lax.ppermute(pieces[piece], "leaf", arrived(1)))

    transposed, norms, near = call(
        self_kernel,
        [shape((rows, dimension), BF16), shape((rows, 128), F32), shape((sides, rows), F32)],
        [points, ordered],
        flops=2 * rows * rows * (dimension + sides),
        exps=rows * rows,
        name="self_tile",
    )
    returns = []
    for step, parts in ((2, two), (1, one)):
        for piece in range(PIECES):
            near, back = call(
                functools.partial(near_kernel, REACH - step),
                [shape((sides, rows), F32), shape((sides, size), BF16)],
                [near_mask, parts[piece], transposed, norms, ordered, near],
                scalars=1,
                flops=2 * rows * size * (dimension + 2 * sides),
                exps=rows * size,
                name="near_tile",
            )
            returns.append(
                lax.ppermute(back, "leaf", [(place + step, place) for place in range(leaves - step)])
            )

    terms = []
    for number, (level, bits) in enumerate(rounds):
        later = rounds[number + 1][1] if number + 1 < len(rounds) else 0
        received = [swapped(messages[0], "leaf", 1 << level)]
        if bits == 2:
            received.append(swapped(messages[1], "leaf", 2 << level))
            received.append(swapped(messages[1], "leaf", 3 << level))
        outs = []
        if bits == 2:
            outs += [shape((dimension, count), BF16)] * 2 + [shape((sides, count), F32)]
        if later == 0:
            outs += [shape((dimension + sides, count), BF16)]
        else:
            outs += [shape((dimension, count), BF16)] + message_shapes(later)
        results = call(
            functools.partial(round_kernel, level, bits, later),
            outs,
            [skeletons, transfer, coords, total] + received,
            flops=8 * dimension * count * count,
            name="join_round",
        )
        results = list(results)
        kept = results[:3] if bits == 2 else []
        terms += list(call(
            functools.partial(sibling_kernel, bits, sides),
            [shape((sides, count), F32)] * bits,
            [coords, received[0]] + kept,
            flops=8 * dimension * count * count,
            exps=2 * count * count,
            name="sibling_terms",
        ))
        results = results[len(kept) :]
        if later:
            coords, messages, total = results[0], results[1:-1], results[-1]
    own_top = results[0]
    tops = [
        lax.ppermute(own_top, "grp", [(place, (place + turn) % groups) for place in range(groups)])
        for turn in range(1, groups)
    ]
    (out,) = call(
        functools.partial(final_kernel, levels, len(tops)),
        [shape((sides, rows), F32)],
        [near, own_top, transfer, leaf_interp] + tops + terms + returns,
        flops=4 * sides * rows * count,
        name="downward",
    )
    return out


def solution(mesh):
    in_specs = (
        P(None, ("leaf", "grp")),
        P(None, ("leaf", "grp")),
        P(("leaf", "grp")),
        P(("leaf", "grp"), None),
        P(("leaf", "grp"), None, None),
        P(None, ("leaf", "grp")),
        P(("leaf", "grp"), None, None, None),
    )
    out_specs = P(None, ("leaf", "grp"))
    return jax.shard_map(local, mesh=mesh, in_specs=in_specs, out_specs=out_specs, check_vma=False)
```

time: 105 us -> 73 us (0.70)
  the two profiles are of different devices: /device:TPU:11 before, /device:TPU:18 now
where the time goes in v1:
time: 73 us; the launch traced here: 72.1 us
  starting transfers between devices  32.8 us (45%)
  waiting for transfers between devices  20.2 us (28%)
  Pallas kernels  12.9 us (18%)
  local copies, waits for them, and re-layouts  5.83 us (8%)
    ppermute x4, starting transfers between devices, local(): lax.ppermute(back, 'leaf', [(place + step, place) for place in range(leav...  14.2 us
    pallas_call x11, Pallas kernels, call(): pl.pallas_call(kernel, out_shape=outs, in_specs=specs, out_specs=[vmem] *...  12.9 us
    ppermute x6, waiting for transfers between devices, swapped(): lax.ppermute(value, axis, [(place, place ^ flip) for place in range(count)])  12.4 us
    ppermute x2, starting transfers between devices, local(): two = [lax.ppermute(piece, 'leaf', arrived(2)) for piece in pieces]  6.99 us
    unnamed x19, local copies, waits for them, and re-layouts  5.83 us
    ppermute x6, starting transfers between devices, swapped(): lax.ppermute(value, axis, [(place, place ^ flip) for place in range(count)])  5.16 us
    ppermute x2, waiting for transfers between devices, local(): two = [lax.ppermute(piece, 'leaf', arrived(2)) for piece in pieces]  3.96 us
    ppermute x4, waiting for transfers between devices, local(): lax.ppermute(back, 'leaf', [(place + step, place) for place in range(leav...  3.91 us
  transfers between devices with their start and end apart: 16, of which 5 were waited for; matrix products, arithmetic and copies ran while one was open for 0% of the time, Pallas kernels for 13%

profile of v1, /device:TPU:18, one launch (start us, length us, event | category | flops | bytes accessed | tf_op | source)
XLA Modules:
  0.0 72.1 jit_solution(1005173275734506285)
XLA Ops:
  0.0 0.7 copy.10
  0.7 0.0 copy-start.8
  0.7 0.7 copy-done.8
  1.4 0.0 copy-start
  1.4 0.9 %copy-done = bf16[1,4,128,128]{3,2,1,0:T(8,128)(2,1)S(1)} copy-done((bf16[1,4,128,128]{3,2,1,0:T(8,128)(2,1)S(1)}, bf16[1,4,128,128]{3,2,1,0:T(8,128)(2,1)}, u32[]{:S(2)}) %copy-start) | copy-done | bytes 131096
  2.3 0.0 copy-start.2
  2.3 0.9 %copy-done.2 = bf16[128,1024]{1,0:T(8,128)(2,1)S(1)} copy-done((bf16[128,1024]{1,0:T(8,128)(2,1)S(1)}, bf16[128,1024]{1,0:T(8,128)(2,1)}, u32[]{:S(2)}) %copy-start.2) | copy-done | bytes 262168
  3.2 0.0 copy-start.4
  3.2 1.0 %copy-done.4 = bf16[256,1024]{1,0:T(8,128)(2,1)S(1)} copy-done((bf16[256,1024]{1,0:T(8,128)(2,1)S(1)}, bf16[256,1024]{1,0:T(8,128)(2,1)}, u32[]{:S(2)}) %copy-start.4) | copy-done | bytes 524312
  4.3 0.0 copy-start.6
  4.3 0.9 %copy-done.6 = bf16[64,1024]{1,0:T(8,128)(2,1)S(1)} copy-done((bf16[64,1024]{1,0:T(8,128)(2,1)S(1)}, bf16[64,1024]{1,0:T(8,128)(2,1)}, u32[]{:S(2)}) %copy-start.6) | copy-done | bytes 131096
  5.2 0.0 copy-start.1
  5.2 1.4 %start.1 = (bf16[320,512]{1,0:T(8,128)(2,1)S(1)}, bf16[320,512]{1,0:T(8,128)(2,1)S(1)}, bf16[64,1024]{1,0:T(8,128)(2,1)S(1)}, bf16[256,128]{1,0:T(8,128)(2,1)S(1...) custom-call(bf16[256,1024]{1,0:T(8,128)(2,1)S(1)} %copy-done.4, ...), custom_call_target="tpu_custom_call" | custom-call | flops 134217728 | bytes 2140672 | tf_op jit(solution)/shard_map/start/pallas_call | solution.py:249
  6.6 0.0 copy-start.5
  6.6 3.6 %collective-permute-start.2 = (bf16[320,512]{1,0:T(8,128)(2,1)S(1)}, bf16[320,512]{1,0:T(8,128)(2,1)S(1)}, u32[]{:S(2)}, u32[]{:S(2)}) collective-permute-start(bf16[320,512]{1,0:T(8,128)(2,1)S(1)} %get-tuple-element.42), channel_id=1, source_target_pairs={{0,4},{2,6},{4,8},{6,10},{8,12},{10,14},{12,16},{14,18},{16,20},{1... | collective-permute-start | bytes 983048 | tf_op jit(solution)/shard_map/ppermute | solution.py:304
  10.2 0.6 collective-permute-start.5
  10.8 2.4 %collective-permute-start.7 = (bf16[400,128]{1,0:T(8,128)(2,1)S(1)}, bf16[400,128]{1,0:T(8,128)(2,1)S(1)}, u32[]{:S(2)}, u32[]{:S(2)}) collective-permute-start(bf16[400,128]{1,0:T(8,128)(2,1)S(1)} %get-tuple-element.51), channel_id=1, source_target_pairs={{0,6},{2,4},{4,2},{6,0},{8,14},{10,12},{12,10},{14,8},{16,22},{18,... | collective-permute-start | bytes 307208 | tf_op jit(solution)/shard_map/ppermute | solution.py:262
  13.2 0.5 collective-permute-start.6
  13.7 3.4 %collective-permute-start.4 = (bf16[320,512]{1,0:T(8,128)(2,1)S(1)}, bf16[320,512]{1,0:T(8,128)(2,1)S(1)}, u32[]{:S(2)}, u32[]{:S(2)}) collective-permute-start(bf16[320,512]{1,0:T(8,128)(2,1)S(1)} %get-tuple-element.38), channel_id=1, source_target_pairs={{0,4},{2,6},{4,8},{6,10},{8,12},{10,14},{12,16},{14,18},{16,20},{1... | collective-permute-start | bytes 983048 | tf_op jit(solution)/shard_map/ppermute | solution.py:304
  17.2 0.0 collective-permute-done.5.refs_0_.first
  17.2 1.3 %collective-permute-start.1 = (bf16[320,512]{1,0:T(8,128)(2,1)S(1)}, bf16[320,512]{1,0:T(8,128)(2,1)S(1)}, u32[]{:S(2)}, u32[]{:S(2)}) collective-permute-start(bf16[320,512]{1,0:T(8,128)(2,1)S(1)} %get-tuple-element.42), channel_id=1, source_target_pairs={{0,2},{4,6},{8,10},{12,14},{16,18},{20,22},{24,26},{28,30},{1,3},{... | collective-permute-start | bytes 983048 | tf_op jit(solution)/shard_map/ppermute | solution.py:308
  18.5 4.0 %collective-permute-done.2.piece = bf16[320,512]{1,0:T(8,128)(2,1)S(1)} collective-permute-done((bf16[320,512]{1,0:T(8,128)(2,1)S(1)}, bf16[320,512]{1,0:T(8,128)(2,1)S(1)}, u32[]{:S(2)}, u32[]{:S(2)}) %collective-permute-start.2) | collective-permute-done | bytes 327712 | tf_op jit(solution)/shard_map/ppermute | solution.py:304
  22.4 3.2 %collective-permute-start.3 = (bf16[320,512]{1,0:T(8,128)(2,1)S(1)}, bf16[320,512]{1,0:T(8,128)(2,1)}, u32[]{:S(2)}, u32[]{:S(2)}) collective-permute-start(bf16[320,512]{1,0:T(8,128)(2,1)S(1)} %collective-permute-done.2.piece), channel_id=1, source_target_pairs={{6,4},{10,8},{14,12},{18,16},{22,20},{26,24},{30,28},{7,5},{11,9},... | collective-permute-start | bytes 983048 | tf_op jit(solution)/shard_map/ppermute | solution.py:309
  25.6 0.0 collective-permute-done.7.refs_2_
  25.6 4.8 %collective-permute-done.6.refs_1_ = bf16[400,128]{1,0:T(8,128)(2,1)S(1)} collective-permute-done((bf16[400,128]{1,0:T(8,128)(2,1)S(1)}, bf16[400,128]{1,0:T(8,128)(2,1)S(1)}, u32[]{:S(2)}, u32[]{:S(2)}) %collective-permute-start.6) | collective-permute-done | bytes 102432 | tf_op jit(solution)/shard_map/ppermute | solution.py:262
  30.4 0.0 copy-done.1
  30.4 0.7 join_round.2
  31.1 1.6 %collective-permute-start.8 = (bf16[384,128]{1,0:T(8,128)(2,1)S(1)}, bf16[384,128]{1,0:T(8,128)(2,1)S(1)}, u32[]{:S(2)}, u32[]{:S(2)}) collective-permute-start(bf16[384,128]{1,0:T(8,128)(2,1)S(1)} %get-tuple-element.54), channel_id=1, source_target_pairs={{0,8},{2,10},{4,12},{6,14},{8,0},{10,2},{12,4},{14,6},{16,24},{18,... | collective-permute-start | bytes 294920 | tf_op jit(solution)/shard_map/ppermute | solution.py:262
  32.7 0.0 collective-permute-start.10
  32.7 4.1 %collective-permute-done.8.refs_0_.first = bf16[384,128]{1,0:T(8,128)(2,1)S(1)} collective-permute-done((bf16[384,128]{1,0:T(8,128)(2,1)S(1)}, bf16[384,128]{1,0:T(8,128)(2,1)S(1)}, u32[]{:S(2)}, u32[]{:S(2)}) %collective-permute-start.8) | collective-permute-done | bytes 98336 | tf_op jit(solution)/shard_map/ppermute | solution.py:262
  36.8 0.0 collective-permute-start.9
  36.8 0.0 copy-done.5
  36.8 2.2 %self_tile.1 = (bf16[1024,256]{1,0:T(8,128)(2,1)S(1)}, f32[1024,128]{1,0:T(8,128)S(1)}, f32[64,1024]{1,0:T(8,128)S(1)}) custom-call(bf16[256,1024]{1,0:T(8,128)(2,1)S(1)} %copy-done.5, bf16[64,1024]{1,0:T(8,128)(2,1)S(1)} %get-tuple-element.39.ordered), custom_call_target="tpu_custom_call" | custom-call | flops 671088640 | bytes 1966080 | tf_op jit(solution)/shard_map/self_tile/pallas_call | solution.py:249
  39.1 3.5 %collective-permute-done.10.refs_2_ = bf16[400,128]{1,0:T(8,128)(2,1)S(1)} collective-permute-done((bf16[400,128]{1,0:T(8,128)(2,1)S(1)}, bf16[400,128]{1,0:T(8,128)(2,1)S(1)}, u32[]{:S(2)}, u32[]{:S(2)}) %collective-permute-start.10) | collective-permute-done | bytes 102432 | tf_op jit(solution)/shard_map/ppermute | solution.py:262
  42.5 1.9 %collective-permute-start = (bf16[320,512]{1,0:T(8,128)(2,1)S(1)}, bf16[320,512]{1,0:T(8,128)(2,1)S(1)}, u32[]{:S(2)}, u32[]{:S(2)}) collective-permute-start(bf16[320,512]{1,0:T(8,128)(2,1)S(1)} %get-tuple-element.38), channel_id=1, source_target_pairs={{0,2},{2,4},{4,6},{6,8},{8,10},{10,12},{12,14},{14,16},{16,18},{18... | collective-permute-start | bytes 983048 | tf_op jit(solution)/shard_map/ppermute | solution.py:315
  44.5 0.0 collective-permute-done.9.refs_1_
  44.5 0.4 join_round.3
  44.8 0.1 collective-permute-start.11
  44.9 0.0 copy-start.7
  44.9 0.6 copy-done.7
  45.6 0.6 near_tile.4
  46.2 0.0 collective-permute-done.4.piece
  46.2 0.6 near_tile.5
  46.8 3.5 %collective-permute-start.13 = (bf16[64,512]{1,0:T(8,128)(2,1)S(1)}, bf16[64,512]{1,0:T(8,128)(2,1)S(1)}, u32[]{:S(2)}, u32[]{:S(2)}) collective-permute-start(bf16[64,512]{1,0:T(8,128)(2,1)S(1)} %get-tuple-element.68), channel_id=1, source_target_pairs={{4,0},{6,2},{8,4},{10,6},{12,8},{14,10},{16,12},{18,14},{20,16},{2... | collective-permute-start | bytes 196616 | tf_op jit(solution)/shard_map/ppermute | solution.py:338
  50.3 0.0 collective-permute-done.1
  50.3 1.9 %collective-permute-start.12 = (bf16[64,512]{1,0:T(8,128)(2,1)S(1)}, bf16[64,512]{1,0:T(8,128)(2,1)S(1)}, u32[]{:S(2)}, u32[]{:S(2)}) collective-permute-start(bf16[64,512]{1,0:T(8,128)(2,1)S(1)} %get-tuple-element.67), channel_id=1, source_target_pairs={{4,0},{6,2},{8,4},{10,6},{12,8},{14,10},{16,12},{18,14},{20,16},{2... | collective-permute-start | bytes 196616 | tf_op jit(solution)/shard_map/ppermute | solution.py:338
  52.3 0.0 collective-permute-done.3
  52.3 1.8 %near_tile.6 = (f32[64,1024]{1,0:T(8,128)S(1)}, bf16[64,512]{1,0:T(8,128)(2,1)S(1)}) custom-call(s32[1,5]{1,0:T(1,128)S(1)} %copy-done.7, bf16[320,512]{1,0:T(8,128)(2,1)S(1)} %broadcast_select_fusion.piece, bf16[1024,256]{1,0:T(8,128)(2,1)S(1)} %get-tuple-element.40.transposed, f32[1024,128]{1,0:T(8,128)S(1)} %get-tuple-element.41.norms, ...), custom_call_target="tpu_custom_call" | custom-call | flops 402653184 | bytes 2097172 | tf_op jit(solution)/shard_map/near_tile/pallas_call | solution.py:249
  54.1 0.0 collective-permute-done.piece
  54.2 1.8 %near_tile.7 = (f32[64,1024]{1,0:T(8,128)S(1)}, bf16[64,512]{1,0:T(8,128)(2,1)S(1)}) custom-call(s32[1,5]{1,0:T(1,128)S(1)} %copy-done.7, bf16[320,512]{1,0:T(8,128)(2,1)S(1)} %collective-permute-done.piece, bf16[1024,256]{1,0:T(8,128)(2,1)S(1)} %get-tuple-element.40.transposed, f32[1024,128]{1,0:T(8,128)S(1)} %get-tuple-element.41.norms, ...), custom_call_target="tpu_custom_call" | custom-call | flops 402653184 | bytes 2097172 | tf_op jit(solution)/shard_map/near_tile/pallas_call | solution.py:249
  56.0 6.8 %collective-permute-start.15 = (bf16[64,512]{1,0:T(8,128)(2,1)S(1)}, bf16[64,512]{1,0:T(8,128)(2,1)S(1)}, u32[]{:S(2)}, u32[]{:S(2)}) collective-permute-start(bf16[64,512]{1,0:T(8,128)(2,1)S(1)} %get-tuple-element.70), channel_id=1, source_target_pairs={{2,0},{4,2},{6,4},{8,6},{10,8},{12,10},{14,12},{16,14},{18,16},{20... | collective-permute-start | bytes 196616 | tf_op jit(solution)/shard_map/ppermute | solution.py:338
  62.8 1.9 %collective-permute-start.14 = (bf16[64,512]{1,0:T(8,128)(2,1)S(1)}, bf16[64,512]{1,0:T(8,128)(2,1)S(1)}, u32[]{:S(2)}, u32[]{:S(2)}) collective-permute-start(bf16[64,512]{1,0:T(8,128)(2,1)S(1)} %get-tuple-element.69), channel_id=1, source_target_pairs={{2,0},{4,2},{6,4},{8,6},{10,8},{12,10},{14,12},{16,14},{18,16},{20... | collective-permute-start | bytes 196616 | tf_op jit(solution)/shard_map/ppermute | solution.py:338
  64.7 0.0 copy-start.3
  64.7 0.6 sibling_terms.2
  65.3 0.6 sibling_terms.3
  65.9 0.0 collective-permute-done.11.refs_0_
  65.9 0.0 collective-permute-done.13.refs_6_
  65.9 0.0 collective-permute-done.12.refs_5_
  65.9 0.0 collective-permute-done.15.refs_8_
  65.9 3.9 %collective-permute-done.14.refs_7_ = bf16[64,512]{1,0:T(8,128)(2,1)S(1)} collective-permute-done((bf16[64,512]{1,0:T(8,128)(2,1)S(1)}, bf16[64,512]{1,0:T(8,128)(2,1)S(1)}, u32[]{:S(2)}, u32[]{:S(2)}) %collective-permute-start.14) | collective-permute-done | bytes 65568 | tf_op jit(solution)/shard_map/ppermute | solution.py:338
  69.8 0.0 copy-done.3
  69.8 2.2 %downward.1 = f32[64,1024]{1,0:T(8,128)} custom-call(f32[64,1024]{1,0:T(8,128)S(1)} %get-tuple-element.47.near, bf16[320,128]{1,0:T(8,128)(2,1)S(1)} %get-tuple-element.56.own_top, bf16[4,128,128]{2,1,0:T(8,128)(2,1)S(1)} %bitcast.8, bf16[128,1024]{1,0:T(8,128)(2,1)S(1)} %copy-done.3, bf16[320,128]{1,0:T(8,128)(2,1)S(1)} %collective-permute-done.11.refs_0_, ...), custom_call_target="tpu_custom_call" | custom-call | flops 33554432 | bytes 1474560 | tf_op jit(solution)/shard_map/downward/pallas_call | solution.py:249
  (1 shorter events, 0.0 us)
Async XLA Ops:
  0.7 0.7 copy-start.8
  1.4 0.9 %copy-start = (bf16[1,4,128,128]{3,2,1,0:T(8,128)(2,1)S(1)}, bf16[1,4,128,128]{3,2,1,0:T(8,128)(2,1)}, u32[]{:S(2)}) copy-start(bf16[1,4,128,128]{3,2,1,0:T(8,128)(2,1)} %param.13) | copy-start | bytes 393220
  2.3 0.9 %copy-start.2 = (bf16[128,1024]{1,0:T(8,128)(2,1)S(1)}, bf16[128,1024]{1,0:T(8,128)(2,1)}, u32[]{:S(2)}) copy-start(bf16[128,1024]{1,0:T(8,128)(2,1)} %interp.3) | copy-start | bytes 786436
  3.2 1.0 %copy-start.4 = (bf16[256,1024]{1,0:T(8,128)(2,1)S(1)}, bf16[256,1024]{1,0:T(8,128)(2,1)}, u32[]{:S(2)}) copy-start(bf16[256,1024]{1,0:T(8,128)(2,1)} %points.3) | copy-start | bytes 1572868
  4.3 0.9 %copy-start.6 = (bf16[64,1024]{1,0:T(8,128)(2,1)S(1)}, bf16[64,1024]{1,0:T(8,128)(2,1)}, u32[]{:S(2)}) copy-start(bf16[64,1024]{1,0:T(8,128)(2,1)} %charges.1) | copy-start | bytes 393220
  5.2 25.2 %copy-start.1 = (bf16[1,4,128,128]{3,2,1,0:T(8,128)(2,1)S(1)}, bf16[1,4,128,128]{3,2,1,0:T(8,128)(2,1)}, u32[]{:S(2)}) copy-start(bf16[1,4,128,128]{3,2,1,0:T(8,128)(2,1)} %param.13) | copy-start | bytes 393220
  6.6 30.2 %copy-start.5 = (bf16[256,1024]{1,0:T(8,128)(2,1)S(1)}, bf16[256,1024]{1,0:T(8,128)(2,1)}, u32[]{:S(2)}) copy-start(bf16[256,1024]{1,0:T(8,128)(2,1)} %points.3) | copy-start | bytes 1572868
  6.6 15.8 %collective-permute-start.2 = (bf16[320,512]{1,0:T(8,128)(2,1)S(1)}, bf16[320,512]{1,0:T(8,128)(2,1)S(1)}, u32[]{:S(2)}, u32[]{:S(2)}) collective-permute-start(bf16[320,512]{1,0:T(8,128)(2,1)S(1)} %get-tuple-element.42), channel_id=1, source_target_pairs={{0,4},{2,6},{4,8},{6,10},{8,12},{10,14},{12,16},{14,18},{16,20},{1... | collective-permute-start | bytes 983048 | tf_op jit(solution)/shard_map/ppermute | solution.py:304
  10.2 7.0 %collective-permute-start.5 = (bf16[384,128]{1,0:T(8,128)(2,1)S(1)}, bf16[384,128]{1,0:T(8,128)(2,1)S(1)}, u32[]{:S(2)}, u32[]{:S(2)}) collective-permute-start(bf16[384,128]{1,0:T(8,128)(2,1)S(1)} %get-tuple-element.50), channel_id=1, source_target_pairs={{0,2},{2,0},{4,6},{6,4},{8,10},{10,8},{12,14},{14,12},{16,18},{18,... | collective-permute-start | bytes 294920 | tf_op jit(solution)/shard_map/ppermute | solution.py:262
  10.8 14.8 %collective-permute-start.7 = (bf16[400,128]{1,0:T(8,128)(2,1)S(1)}, bf16[400,128]{1,0:T(8,128)(2,1)S(1)}, u32[]{:S(2)}, u32[]{:S(2)}) collective-permute-start(bf16[400,128]{1,0:T(8,128)(2,1)S(1)} %get-tuple-element.51), channel_id=1, source_target_pairs={{0,6},{2,4},{4,2},{6,0},{8,14},{10,12},{12,10},{14,8},{16,22},{18,... | collective-permute-start | bytes 307208 | tf_op jit(solution)/shard_map/ppermute | solution.py:262
  13.2 17.2 %collective-permute-start.6 = (bf16[400,128]{1,0:T(8,128)(2,1)S(1)}, bf16[400,128]{1,0:T(8,128)(2,1)S(1)}, u32[]{:S(2)}, u32[]{:S(2)}) collective-permute-start(bf16[400,128]{1,0:T(8,128)(2,1)S(1)} %get-tuple-element.51), channel_id=1, source_target_pairs={{0,4},{2,6},{4,0},{6,2},{8,12},{10,14},{12,8},{14,10},{16,20},{18,... | collective-permute-start | bytes 307208 | tf_op jit(solution)/shard_map/ppermute | solution.py:262
  13.7 32.4 %collective-permute-start.4 = (bf16[320,512]{1,0:T(8,128)(2,1)S(1)}, bf16[320,512]{1,0:T(8,128)(2,1)S(1)}, u32[]{:S(2)}, u32[]{:S(2)}) collective-permute-start(bf16[320,512]{1,0:T(8,128)(2,1)S(1)} %get-tuple-element.38), channel_id=1, source_target_pairs={{0,4},{2,6},{4,8},{6,10},{8,12},{10,14},{12,16},{14,18},{16,20},{1... | collective-permute-start | bytes 983048 | tf_op jit(solution)/shard_map/ppermute | solution.py:304
  17.2 33.1 %collective-permute-start.1 = (bf16[320,512]{1,0:T(8,128)(2,1)S(1)}, bf16[320,512]{1,0:T(8,128)(2,1)S(1)}, u32[]{:S(2)}, u32[]{:S(2)}) collective-permute-start(bf16[320,512]{1,0:T(8,128)(2,1)S(1)} %get-tuple-element.42), channel_id=1, source_target_pairs={{0,2},{4,6},{8,10},{12,14},{16,18},{20,22},{24,26},{28,30},{1,3},{... | collective-permute-start | bytes 983048 | tf_op jit(solution)/shard_map/ppermute | solution.py:308
  22.4 29.8 %collective-permute-start.3 = (bf16[320,512]{1,0:T(8,128)(2,1)S(1)}, bf16[320,512]{1,0:T(8,128)(2,1)}, u32[]{:S(2)}, u32[]{:S(2)}) collective-permute-start(bf16[320,512]{1,0:T(8,128)(2,1)S(1)} %collective-permute-done.2.piece), channel_id=1, source_target_pairs={{6,4},{10,8},{14,12},{18,16},{22,20},{26,24},{30,28},{7,5},{11,9},... | collective-permute-start | bytes 983048 | tf_op jit(solution)/shard_map/ppermute | solution.py:309
  31.1 5.7 %collective-permute-start.8 = (bf16[384,128]{1,0:T(8,128)(2,1)S(1)}, bf16[384,128]{1,0:T(8,128)(2,1)S(1)}, u32[]{:S(2)}, u32[]{:S(2)}) collective-permute-start(bf16[384,128]{1,0:T(8,128)(2,1)S(1)} %get-tuple-element.54), channel_id=1, source_target_pairs={{0,8},{2,10},{4,12},{6,14},{8,0},{10,2},{12,4},{14,6},{16,24},{18,... | collective-permute-start | bytes 294920 | tf_op jit(solution)/shard_map/ppermute | solution.py:262
  32.7 9.8 %collective-permute-start.10 = (bf16[400,128]{1,0:T(8,128)(2,1)S(1)}, bf16[400,128]{1,0:T(8,128)(2,1)S(1)}, u32[]{:S(2)}, u32[]{:S(2)}) collective-permute-start(bf16[400,128]{1,0:T(8,128)(2,1)S(1)} %get-tuple-element.55), channel_id=1, source_target_pairs={{0,24},{2,26},{4,28},{6,30},{8,16},{10,18},{12,20},{14,22},{16,8},... | collective-permute-start | bytes 307208 | tf_op jit(solution)/shard_map/ppermute | solution.py:262
  36.8 7.7 %collective-permute-start.9 = (bf16[400,128]{1,0:T(8,128)(2,1)S(1)}, bf16[400,128]{1,0:T(8,128)(2,1)S(1)}, u32[]{:S(2)}, u32[]{:S(2)}) collective-permute-start(bf16[400,128]{1,0:T(8,128)(2,1)S(1)} %get-tuple-element.55), channel_id=1, source_target_pairs={{0,16},{2,18},{4,20},{6,22},{8,24},{10,26},{12,28},{14,30},{16,0},... | collective-permute-start | bytes 307208 | tf_op jit(solution)/shard_map/ppermute | solution.py:262
  42.5 11.6 %collective-permute-start = (bf16[320,512]{1,0:T(8,128)(2,1)S(1)}, bf16[320,512]{1,0:T(8,128)(2,1)S(1)}, u32[]{:S(2)}, u32[]{:S(2)}) collective-permute-start(bf16[320,512]{1,0:T(8,128)(2,1)S(1)} %get-tuple-element.38), channel_id=1, source_target_pairs={{0,2},{2,4},{4,6},{6,8},{8,10},{10,12},{12,14},{14,16},{16,18},{18... | collective-permute-start | bytes 983048 | tf_op jit(solution)/shard_map/ppermute | solution.py:315
  44.8 21.1 %collective-permute-start.11 = (bf16[320,128]{1,0:T(8,128)(2,1)S(1)}, bf16[320,128]{1,0:T(8,128)(2,1)S(1)}, u32[]{:S(2)}, u32[]{:S(2)}) collective-permute-start(bf16[320,128]{1,0:T(8,128)(2,1)S(1)} %get-tuple-element.56.own_top), channel_id=1, source_target_pairs={{0,1},{1,0},{2,3},{3,2},{4,5},{5,4},{6,7},{7,6},{8,9},{9,8},{10,11... | collective-permute-start | bytes 245768 | tf_op jit(solution)/shard_map/ppermute | solution.py:377
  44.9 0.7 copy-start.7
  46.8 19.1 %collective-permute-start.13 = (bf16[64,512]{1,0:T(8,128)(2,1)S(1)}, bf16[64,512]{1,0:T(8,128)(2,1)S(1)}, u32[]{:S(2)}, u32[]{:S(2)}) collective-permute-start(bf16[64,512]{1,0:T(8,128)(2,1)S(1)} %get-tuple-element.68), channel_id=1, source_target_pairs={{4,0},{6,2},{8,4},{10,6},{12,8},{14,10},{16,12},{18,14},{20,16},{2... | collective-permute-start | bytes 196616 | tf_op jit(solution)/shard_map/ppermute | solution.py:338
  50.3 15.6 %collective-permute-start.12 = (bf16[64,512]{1,0:T(8,128)(2,1)S(1)}, bf16[64,512]{1,0:T(8,128)(2,1)S(1)}, u32[]{:S(2)}, u32[]{:S(2)}) collective-permute-start(bf16[64,512]{1,0:T(8,128)(2,1)S(1)} %get-tuple-element.67), channel_id=1, source_target_pairs={{4,0},{6,2},{8,4},{10,6},{12,8},{14,10},{16,12},{18,14},{20,16},{2... | collective-permute-start | bytes 196616 | tf_op jit(solution)/shard_map/ppermute | solution.py:338
  56.0 9.9 %collective-permute-start.15 = (bf16[64,512]{1,0:T(8,128)(2,1)S(1)}, bf16[64,512]{1,0:T(8,128)(2,1)S(1)}, u32[]{:S(2)}, u32[]{:S(2)}) collective-permute-start(bf16[64,512]{1,0:T(8,128)(2,1)S(1)} %get-tuple-element.70), channel_id=1, source_target_pairs={{2,0},{4,2},{6,4},{8,6},{10,8},{12,10},{14,12},{16,14},{18,16},{20... | collective-permute-start | bytes 196616 | tf_op jit(solution)/shard_map/ppermute | solution.py:338
  62.8 7.1 %collective-permute-start.14 = (bf16[64,512]{1,0:T(8,128)(2,1)S(1)}, bf16[64,512]{1,0:T(8,128)(2,1)S(1)}, u32[]{:S(2)}, u32[]{:S(2)}) collective-permute-start(bf16[64,512]{1,0:T(8,128)(2,1)S(1)} %get-tuple-element.69), channel_id=1, source_target_pairs={{2,0},{4,2},{6,4},{8,6},{10,8},{12,10},{14,12},{16,14},{18,16},{20... | collective-permute-start | bytes 196616 | tf_op jit(solution)/shard_map/ppermute | solution.py:338
  64.7 5.1 %copy-start.3 = (bf16[128,1024]{1,0:T(8,128)(2,1)S(1)}, bf16[128,1024]{1,0:T(8,128)(2,1)}, u32[]{:S(2)}) copy-start(bf16[128,1024]{1,0:T(8,128)(2,1)} %interp.3) | copy-start | bytes 786436

commit v2 on v1

v2 whole, which is shorter than its diff:
```python
import functools

import jax
import jax.numpy as jnp
from jax import lax
from jax.experimental import pallas as pl
from jax.experimental.pallas import tpu as pltpu
from jax.sharding import PartitionSpec as P

REACH = 2
BF16 = jnp.bfloat16
F32 = jnp.float32
LOG2E = 1.4426950408889634
HIGHEST = lax.Precision.HIGHEST
PAD = 16
VMEM_LIMIT = 40 * 1024 * 1024
START_VMEM = 56 * 1024 * 1024

NN = ((1,), (0,))
NT = ((1,), (1,))
TN = ((0,), (0,))


def dot(left, right, contract=NN, precision=None):
    return lax.dot_general(
        left, right, (contract, ((), ())), preferred_element_type=F32, precision=precision
    )


def halves(value):
    high = value.astype(BF16)
    return high, (value - high.astype(F32)).astype(BF16)


def row_norms(points):
    wide = points.astype(F32)
    return jnp.sum(wide * wide, axis=0, keepdims=True)


def column_norms(points):
    wide = points.astype(F32)
    high, low = halves(wide * wide)
    ones = jnp.ones((points.shape[0], 128), BF16)
    return dot(high, ones, TN) + dot(low, ones, TN)


def one_hot(index, rows, first):
    place = lax.broadcasted_iota(jnp.int32, (rows, index.shape[1]), 0) + first
    return jnp.where(place == index, 1.0, 0.0).astype(BF16)


def small_kernel(source, target):
    scale = 2.0 * LOG2E / source.shape[0]
    inner = dot(source, target, TN)
    squares = column_norms(source)[:, : target.shape[1]] + row_norms(target)
    return jnp.exp2(scale * (2.0 * inner - squares))


def pick(first, second, index, bit):
    count = first.shape[1]
    table = jnp.concatenate(
        [one_hot(index, count, count * bit), one_hot(index, count, count * (1 - bit))], axis=0
    )
    return dot(jnp.concatenate([first, second], axis=1), table).astype(BF16)


def write_messages(weights, coords, transfers, index, near_row, near_ref, far_ref, sum_ref):
    dimension, (sides, count) = coords.shape[0], weights.shape
    first = transfers[0].astype(F32)
    once = dot(weights, first, NT, HIGHEST)
    summed = once
    if len(transfers) == 2:
        summed = dot(once, transfers[1].astype(F32), NT, HIGHEST)
    for ref, own, row in ((near_ref, weights, near_row), (far_ref, once, index)):
        if ref is not None:
            ref[:dimension] = coords
            ref[dimension : dimension + sides] = own.astype(BF16)
            ref[dimension + sides : dimension + 2 * sides] = summed.astype(BF16)
            ref[dimension + 2 * sides :] = jnp.broadcast_to(
                row.astype(F32), (PAD, count)
            ).astype(BF16)
    sum_ref[...] = summed


def start_kernel(bits, *refs):
    inputs, outs = refs[:7], refs[7 : 10 + bits]
    held, sems = refs[10 + bits : -1], refs[-1]
    copies = [
        pltpu.make_async_copy(source, target, sems.at[number])
        for number, (source, target) in enumerate(zip(inputs, held))
    ]
    for copy in copies:
        copy.start()
    order, skeletons, mask, charges, points, interp, transfer = held
    ordered_ref, coords_ref, messages = outs[0], outs[1], outs[2:]
    rows = points.shape[1]
    for copy in copies[:4]:
        copy.wait()
    width = rows // 4
    for column in range(0, rows, width):
        table = one_hot(order[:, column : column + width], rows, 0)
        ordered_ref[:, column : column + width] = dot(charges[...], table).astype(BF16)
    copies[4].wait()
    coords = dot(points[...], one_hot(skeletons[0], rows, 0)).astype(BF16)
    coords_ref[...] = coords
    copies[5].wait()
    weights = dot(ordered_ref[...], interp[...], NT)
    copies[6].wait()
    write_messages(
        weights,
        coords,
        [transfer[level] for level in range(bits)],
        skeletons[1],
        jnp.broadcast_to(mask[:, 1:2], (1, coords.shape[1])),
        messages[0],
        messages[1] if bits == 2 else None,
        messages[-1],
    )


def pack_kernel(points, ordered, tall_ref, wide_ref):
    dimension, rows = points.shape
    sides = ordered.shape[0]
    wide_ref[:dimension] = points[...]
    wide_ref[dimension:] = ordered[...]
    tall_ref[:rows] = jnp.transpose(points[...])
    for number in range(rows // dimension):
        tall_ref[rows + number * sides : rows + (number + 1) * sides] = ordered[
            :, number * dimension : (number + 1) * dimension
        ]


def round_kernel(level, bits, later, skeletons, transfer, coords, total, *refs):
    position = lax.axis_index("leaf")
    dimension, count = coords.shape
    sides = total.shape[0]
    low = (position >> level) & 1
    if bits == 2:
        first, second, third = (ref[...] for ref in refs[:3])
        coords_up_ref, sibling_coords_ref, sibling_weights_ref = refs[3:6]
        outs = refs[6:]
        high = (position >> (level + 1)) & 1
        middle = pick(coords[...], first[:dimension], skeletons[level + 1], low)
        row = dimension + 2 * sides
        index = second[row : row + 1].astype(F32).astype(jnp.int32)
        sibling = pick(second[:dimension], third[:dimension], index, low)
        coords_up_ref[...] = middle
        sibling_coords_ref[...] = sibling
        span = slice(dimension, dimension + sides)
        sibling_weights_ref[...] = second[span].astype(F32) + third[span].astype(F32)
        top = pick(middle, sibling, skeletons[level + 2], high)
        span = slice(dimension + sides, dimension + 2 * sides)
        weights = (
            (total[...] + first[span].astype(F32))
            + (second[span].astype(F32) + third[span].astype(F32))
        )
    else:
        first = refs[0][...]
        outs = refs[1:]
        top = pick(coords[...], first[:dimension], skeletons[level + 1], low)
        weights = total[...] + first[dimension + sides : dimension + 2 * sides].astype(F32)
    level += bits
    if later == 0:
        outs[0][:dimension] = top
        outs[0][dimension:] = weights.astype(BF16)
        return
    outs[0][...] = top
    write_messages(
        weights,
        top,
        [transfer[level + step] for step in range(later)],
        skeletons[level + 1],
        skeletons[level + 1],
        outs[1],
        outs[2] if later == 2 else None,
        outs[-1],
    )


def sibling_kernel(bits, sides, coords, first, *refs):
    dimension = coords.shape[0]
    weights = first[dimension : dimension + sides].astype(F32)
    refs[-bits][...] = dot(weights, small_kernel(first[:dimension], coords[...]), NN, HIGHEST)
    if bits == 2:
        coords_up, sibling_coords, sibling_weights = refs[:3]
        refs[-1][...] = dot(
            sibling_weights[...], small_kernel(sibling_coords[...], coords_up[...]), NN, HIGHEST
        )


def tall_norms(tall):
    high, low = halves(jnp.square(tall.astype(F32)))
    ones = jnp.ones((tall.shape[1], 128), BF16)
    return dot(high, ones) + dot(low, ones)


def tall_charges(tall, rows, start):
    dimension = tall.shape[1]
    sides = (tall.shape[0] - rows) * dimension // rows
    first = rows + start // dimension * sides
    return tall[first : first + sides]


def bands(tall, wide):
    dimension = tall.shape[1]
    rows = wide.shape[1]
    scale = 2.0 * LOG2E / dimension
    target_norms = row_norms(wide[:dimension]) * scale
    for row in range(0, rows, dimension):
        band = slice(row, row + dimension)
        source = tall[band]
        inner = dot(source, wide[:dimension])
        squares = jnp.tile(tall_norms(source) * scale, (1, rows // 128)) + target_norms
        yield band, jnp.exp2((2.0 * scale) * inner - squares).astype(BF16)


def self_kernel(tall, wide, near_ref):
    dimension = tall.shape[1]
    for band, tile in bands(tall, wide):
        near_ref[:, band] = dot(wide[dimension:], tile, NT)


def near_kernel(mask, own_tall, own_wide, tall, wide, message, near, near_ref, back_ref, side_ref, held):
    dimension = own_tall.shape[1]
    rows = near.shape[1]
    sides = near.shape[0]
    odd = lax.rem(lax.axis_index("leaf"), 2)
    near_ref[...] = near[...]
    held[...] = jnp.zeros_like(held)

    @pl.when(mask[0, 0] > 0)
    def _():
        total = near[...]
        for band, tile in bands(tall, own_wide):
            total = total + dot(tall_charges(tall, rows, band.start), tile)
            held[:, band] = dot(own_wide[dimension:], tile, NT)
        near_ref[...] = total

    def pair(source, sum_ref):
        total = None
        for band, tile in bands(source, wide):
            sum_ref[:, band] += dot(wide[dimension:], tile, NT)
            part = dot(tall_charges(source, rows, band.start), tile)
            total = part if total is None else total + part
        side_ref[...] = total.astype(BF16)

    first = dimension + 2 * sides
    across = jnp.max(message[first : first + PAD].astype(F32)) > 0.5
    with_next = mask[0, REACH + 1] > 0
    go_odd = jnp.logical_and(odd == 1, across)
    go_even = jnp.logical_and(odd == 0, with_next)

    @pl.when(go_odd)
    def _():
        pair(tall, held)

    @pl.when(go_even)
    def _():
        pair(own_tall, near_ref)

    @pl.when(jnp.logical_not(jnp.logical_or(go_odd, go_even)))
    def _():
        side_ref[...] = jnp.zeros_like(side_ref)

    back_ref[...] = held[...].astype(BF16)


def far_kernel(levels, others, own_top, transfer, interp, *refs):
    tops, terms, out_ref = refs[:others], refs[others:-1], refs[-1]
    sides = out_ref.shape[0]
    dimension = own_top.shape[0] - sides
    potential = None
    for top in tops:
        part = dot(
            top[dimension:].astype(F32),
            small_kernel(top[:dimension], own_top[:dimension]),
            NN,
            HIGHEST,
        )
        potential = part if potential is None else potential + part
    for level in range(levels, 0, -1):
        term = terms[level - 1][...]
        if potential is not None:
            term = term + dot(potential, transfer[level - 1].astype(F32), NN, HIGHEST)
        potential = term
    high, low = halves(potential)
    out_ref[...] = dot(high, interp[...]) + dot(low, interp[...])


def sum_kernel(near, far, back, side, out_ref):
    out_ref[...] = (near[...] + far[...]) + (back[...].astype(F32) + side[...].astype(F32))


def call(kernel, outs, args, scalars=0, scratch=(), anywhere=False, flops=0, exps=0, name=None):
    vmem = pl.BlockSpec(memory_space=pltpu.VMEM)
    smem = pl.BlockSpec(memory_space=pltpu.SMEM)
    rest = pl.BlockSpec(memory_space=pl.ANY) if anywhere else vmem
    specs = [smem] * scalars + [rest] * (len(args) - scalars)
    moved = 0 if anywhere else sum(a.size * a.dtype.itemsize for a in list(args) + list(outs))
    return pl.pallas_call(
        kernel,
        out_shape=outs,
        in_specs=specs,
        out_specs=[vmem] * len(outs),
        scratch_shapes=list(scratch),
        compiler_params=pltpu.CompilerParams(
            vmem_limit_bytes=START_VMEM if anywhere else VMEM_LIMIT
        ),
        cost_estimate=pl.CostEstimate(flops=flops, bytes_accessed=moved, transcendentals=exps),
        name=name,
    )(*args)


def swapped(value, axis, flip):
    count = lax.axis_size(axis)
    return lax.ppermute(value, axis, [(place, place ^ flip) for place in range(count)])


def rotated(value, axis, turn):
    count = lax.axis_size(axis)
    return lax.ppermute(value, axis, [(place, (place + turn) % count) for place in range(count)])


def shape(dims, dtype):
    return jax.ShapeDtypeStruct(dims, dtype)


def local(points, charges, order, near_mask, skeletons, leaf_interp, transfer):
    dimension, rows = points.shape
    sides, count = charges.shape[0], leaf_interp.shape[0]
    leaves, groups = lax.axis_size("leaf"), lax.axis_size("grp")
    levels = leaves.bit_length() - 1
    rounds = []
    level = 0
    while level < levels:
        rounds.append((level, min(2, levels - level)))
        level += rounds[-1][1]
    message = shape((dimension + 2 * sides + PAD, count), BF16)

    def message_shapes(bits):
        return [message] * bits + [shape((sides, count), F32)]

    bits = rounds[0][1]
    skeletons = jnp.transpose(skeletons, (1, 0, 2))
    transfer = transfer[0]
    inputs = [order.reshape(1, rows), skeletons, near_mask, charges, points, leaf_interp, transfer]
    ordered, coords, *messages, total = call(
        functools.partial(start_kernel, bits),
        [shape((sides, rows), BF16), shape((dimension, count), BF16)] + message_shapes(bits),
        inputs,
        scratch=[pltpu.VMEM(value.shape, value.dtype) for value in inputs]
        + [pltpu.SemaphoreType.DMA((len(inputs),))],
        anywhere=True,
        name="start",
    )

    def exchange(level, bits):
        received = [swapped(messages[0], "leaf", 1 << level)]
        if bits == 2:
            received.append(swapped(messages[1], "leaf", 2 << level))
            received.append(swapped(messages[1], "leaf", 3 << level))
        return received

    received = exchange(0, bits)

    own_tall, own_wide = call(
        pack_kernel,
        [
            shape((rows + sides * rows // dimension, dimension), BF16),
            shape((dimension + sides, rows), BF16),
        ],
        [points, ordered],
        flops=dimension * rows,
        name="pack",
    )
    (near,) = call(
        self_kernel,
        [shape((sides, rows), F32)],
        [own_tall, own_wide],
        flops=2 * rows * rows * (dimension + sides),
        exps=rows * rows,
        name="self_tile",
    )
    own_tall, own_wide, near, received = lax.optimization_barrier(
        (own_tall, own_wide, near, received)
    )
    first_message = received[0]
    tall = rotated(own_tall, "leaf", 2)
    wide = swapped(own_wide, "leaf", 1)
    near, back, side = call(
        near_kernel,
        [shape((sides, rows), F32), shape((sides, rows), BF16), shape((sides, rows), BF16)],
        [near_mask, own_tall, own_wide, tall, wide, first_message, near],
        scalars=1,
        scratch=[pltpu.VMEM((sides, rows), F32)],
        flops=4 * rows * rows * (dimension + 2 * sides),
        exps=2 * rows * rows,
        name="near_tiles",
    )
    back = rotated(back, "leaf", -2)
    side = swapped(side, "leaf", 1)

    terms = []
    for number, (level, bits) in enumerate(rounds):
        later = rounds[number + 1][1] if number + 1 < len(rounds) else 0
        if number:
            received = exchange(level, bits)
        outs = []
        if bits == 2:
            outs += [shape((dimension, count), BF16)] * 2 + [shape((sides, count), F32)]
        if later == 0:
            outs += [shape((dimension + sides, count), BF16)]
        else:
            outs += [shape((dimension, count), BF16)] + message_shapes(later)
        results = list(
            call(
                functools.partial(round_kernel, level, bits, later),
                outs,
                [skeletons, transfer, coords, total] + received,
                flops=8 * dimension * count * count,
                name="join_round",
            )
        )
        kept = results[:3] if bits == 2 else []
        terms += list(
            call(
                functools.partial(sibling_kernel, bits, sides),
                [shape((sides, count), F32)] * bits,
                [coords, received[0]] + kept,
                flops=8 * dimension * count * count,
                exps=2 * count * count,
                name="sibling_terms",
            )
        )
        results = results[len(kept) :]
        if later:
            coords, messages, total = results[0], results[1:-1], results[-1]
    own_top = results[0]
    tops = [rotated(own_top, "grp", turn) for turn in range(1, groups)]
    (far,) = call(
        functools.partial(far_kernel, levels, len(tops)),
        [shape((sides, rows), F32)],
        [own_top, transfer, leaf_interp] + tops + terms,
        flops=4 * sides * rows * count,
        name="far_field",
    )
    (out,) = call(
        sum_kernel,
        [shape((sides, rows), F32)],
        [near, far, back, side],
        flops=3 * sides * rows,
        name="total",
    )
    return out


def solution(mesh):
    in_specs = (
        P(None, ("leaf", "grp")),
        P(None, ("leaf", "grp")),
        P(("leaf", "grp")),
        P(("leaf", "grp"), None),
        P(("leaf", "grp"), None, None),
        P(None, ("leaf", "grp")),
        P(("leaf", "grp"), None, None, None),
    )
    out_specs = P(None, ("leaf", "grp"))
    return jax.shard_map(local, mesh=mesh, in_specs=in_specs, out_specs=out_specs, check_vma=False)
```

time: 73 us -> 48.2 us (0.66)
  the two profiles are of different devices: /device:TPU:18 before, /device:TPU:16 now
where the time goes in v2:
time: 48.2 us; the launch traced here: 47.8 us
  waiting for transfers between devices  20.2 us (42%)
  starting transfers between devices  15.2 us (32%)
  Pallas kernels  11.4 us (24%)
  local copies, waits for them, and re-layouts  0.94 us (2%)
    ppermute x3, waiting for transfers between devices, rotated(): lax.ppermute(value, axis, [(place, (place + turn) % count) for place in r...  16.3 us
    pallas_call x10, Pallas kernels, call(): pl.pallas_call(kernel, out_shape=outs, in_specs=specs, out_specs=[vmem] *...  11.4 us
    ppermute x8, starting transfers between devices, swapped(): lax.ppermute(value, axis, [(place, place ^ flip) for place in range(count)])  8.92 us
    ppermute x3, starting transfers between devices, rotated(): lax.ppermute(value, axis, [(place, (place + turn) % count) for place in r...  6.3 us
    ppermute x8, waiting for transfers between devices, swapped(): lax.ppermute(value, axis, [(place, place ^ flip) for place in range(count)])  3.91 us
  transfers between devices with their start and end apart: 11, of which 5 were waited for; matrix products, arithmetic and copies ran while one was open for 0% of the time, Pallas kernels for 15%

profile of v2, /device:TPU:16, one launch (start us, length us, event | category | flops | bytes accessed | tf_op | source)
XLA Modules:
  0.0 47.8 jit_solution(14501776445176343747)
XLA Ops:
  0.0 0.0 copy-start
  0.0 3.5 %start.1 = (bf16[64,1024]{1,0:T(8,128)(2,1)}, bf16[256,128]{1,0:T(8,128)(2,1)}, bf16[400,128]{1,0:T(8,128)(2,1)}, bf16[400,128]{1,0:T(8,128)(2,1)}, f32[64,128]{1,0:T(8,128)}) custom-call(s32[1,1024]{1,0:T(1,128)} %bitcast.10, s32[5,1,128]{2,1,0:T(1,128)} %bitcast.7, s32[1,5]{1,0:T(1,128)} %mask.1, bf16[64,1024]{1,0:T(8,128)(2,1)} %refs_3_.1, ...), custom_call_target="tpu_custom_call" | custom-call | tf_op jit(solution)/shard_map/start/pallas_call | solution.py:300
  3.5 1.6 %collective-permute-start = (bf16[400,128]{1,0:T(8,128)(2,1)}, bf16[400,128]{1,0:T(8,128)(2,1)S(1)}, u32[]{:S(2)}, u32[]{:S(2)}) collective-permute-start(bf16[400,128]{1,0:T(8,128)(2,1)} %get-tuple-element.39), channel_id=1, source_target_pairs={{0,2},{2,0},{4,6},{6,4},{8,10},{10,8},{12,14},{14,12},{16,18},{18,... | collective-permute-start | bytes 307208 | tf_op jit(solution)/shard_map/ppermute | solution.py:316
  5.0 1.5 %collective-permute-start.2 = (bf16[400,128]{1,0:T(8,128)(2,1)}, bf16[400,128]{1,0:T(8,128)(2,1)S(1)}, u32[]{:S(2)}, u32[]{:S(2)}) collective-permute-start(bf16[400,128]{1,0:T(8,128)(2,1)} %get-tuple-element.40), channel_id=1, source_target_pairs={{0,6},{2,4},{4,2},{6,0},{8,14},{10,12},{12,10},{14,8},{16,22},{18,... | collective-permute-start | bytes 307208 | tf_op jit(solution)/shard_map/ppermute | solution.py:316
  6.5 0.5 %collective-permute-start.1 = (bf16[400,128]{1,0:T(8,128)(2,1)}, bf16[400,128]{1,0:T(8,128)(2,1)S(1)}, u32[]{:S(2)}, u32[]{:S(2)}) collective-permute-start(bf16[400,128]{1,0:T(8,128)(2,1)} %get-tuple-element.40), channel_id=1, source_target_pairs={{0,4},{2,6},{4,0},{6,2},{8,12},{10,14},{12,8},{14,10},{16,20},{18,... | collective-permute-start | bytes 307208 | tf_op jit(solution)/shard_map/ppermute | solution.py:316
  7.0 0.0 copy-done
  7.0 0.0 copy-start.4
  7.0 0.9 %copy-done.4 = bf16[64,1024]{1,0:T(8,128)(2,1)S(1)} copy-done((bf16[64,1024]{1,0:T(8,128)(2,1)S(1)}, bf16[64,1024]{1,0:T(8,128)(2,1)}, u32[]{:S(2)}) %copy-start.4) | copy-done | bytes 131096
  7.9 0.2 pack.1
  8.1 0.0 copy-start.1
  8.1 0.0 copy-start.3
  8.2 0.0 copy-start.5
  8.2 2.4 %self_tile.1.near = f32[64,1024]{1,0:T(8,128)S(1)} custom-call(bf16[1280,256]{1,0:T(8,128)(2,1)S(1)} %get-tuple-element.41.tall.own_tall, bf16[320,1024]{1,0:T(8,128)(2,1)S(1)} %get-tuple-element.42.wide.own_wide), custom_call_target="tpu_custom_call" | custom-call | flops 671088640 | bytes 1572864 | tf_op jit(solution)/shard_map/self_tile/pallas_call | solution.py:300
  10.6 0.0 copy-start.6
  10.6 0.0 collective-permute-done.message.refs_0_.first
  10.6 1.0 %collective-permute-done.2.refs_2_ = bf16[400,128]{1,0:T(8,128)(2,1)S(1)} collective-permute-done((bf16[400,128]{1,0:T(8,128)(2,1)}, bf16[400,128]{1,0:T(8,128)(2,1)S(1)}, u32[]{:S(2)}, u32[]{:S(2)}) %collective-permute-start.2) | collective-permute-done | bytes 102432 | tf_op jit(solution)/shard_map/ppermute | solution.py:316
  11.7 1.2 %collective-permute-done.1.refs_1_ = bf16[400,128]{1,0:T(8,128)(2,1)S(1)} collective-permute-done((bf16[400,128]{1,0:T(8,128)(2,1)}, bf16[400,128]{1,0:T(8,128)(2,1)S(1)}, u32[]{:S(2)}, u32[]{:S(2)}) %collective-permute-start.1) | collective-permute-done | bytes 102432 | tf_op jit(solution)/shard_map/ppermute | solution.py:316
  12.8 0.7 %collective-permute-start.3 = (bf16[1280,256]{1,0:T(8,128)(2,1)S(1)}, bf16[1280,256]{1,0:T(8,128)(2,1)S(1)}, u32[]{:S(2)}, u32[]{:S(2)}) collective-permute-start(bf16[1280,256]{1,0:T(8,128)(2,1)S(1)} %get-tuple-element.41.tall.own_tall), channel_id=1, source_target_pairs={{0,4},{2,6},{4,8},{6,10},{8,12},{10,14},{12,16},{14,18},{16,20},{1... | collective-permute-start | bytes 1966088 | tf_op jit(solution)/shard_map/ppermute | solution.py:321
  13.5 1.4 %collective-permute-start.4 = (bf16[320,1024]{1,0:T(8,128)(2,1)S(1)}, bf16[320,1024]{1,0:T(8,128)(2,1)S(1)}, u32[]{:S(2)}, u32[]{:S(2)}) collective-permute-start(bf16[320,1024]{1,0:T(8,128)(2,1)S(1)} %get-tuple-element.42.wide.own_wide), channel_id=1, source_target_pairs={{0,2},{2,0},{4,6},{6,4},{8,10},{10,8},{12,14},{14,12},{16,18},{18,... | collective-permute-start | bytes 1966088 | tf_op jit(solution)/shard_map/ppermute | solution.py:316
  14.9 0.0 copy-done.1
  14.9 0.0 copy-done.3
  14.9 0.0 copy-done.5
  14.9 0.0 copy-done.6
  14.9 0.7 %join_round.2 = (bf16[256,128]{1,0:T(8,128)(2,1)S(1)}, bf16[256,128]{1,0:T(8,128)(2,1)S(1)}, f32[64,128]{1,0:T(8,128)S(1)}, bf16[256,128]{1,0:T(8,128)(2,1)S(1)}...) custom-call(s32[5,1,128]{2,1,0:T(1,128)S(1)} %bitcast.8, ...), custom_call_target="tpu_custom_call" | custom-call | flops 33554432 | bytes 1006080 | tf_op jit(solution)/shard_map/join_round/pallas_call | solution.py:300
  15.6 0.0 copy-start.7
  15.6 0.5 %collective-permute-start.7 = (bf16[400,128]{1,0:T(8,128)(2,1)S(1)}, bf16[400,128]{1,0:T(8,128)(2,1)S(1)}, u32[]{:S(2)}, u32[]{:S(2)}) collective-permute-start(bf16[400,128]{1,0:T(8,128)(2,1)S(1)} %get-tuple-element.53), channel_id=1, source_target_pairs={{0,24},{2,26},{4,28},{6,30},{8,16},{10,18},{12,20},{14,22},{16,8},... | collective-permute-start | bytes 307208 | tf_op jit(solution)/shard_map/ppermute | solution.py:316
  16.1 3.5 %collective-permute-start.6 = (bf16[400,128]{1,0:T(8,128)(2,1)S(1)}, bf16[400,128]{1,0:T(8,128)(2,1)S(1)}, u32[]{:S(2)}, u32[]{:S(2)}) collective-permute-start(bf16[400,128]{1,0:T(8,128)(2,1)S(1)} %get-tuple-element.53), channel_id=1, source_target_pairs={{0,16},{2,18},{4,20},{6,22},{8,24},{10,26},{12,28},{14,30},{16,0},... | collective-permute-start | bytes 307208 | tf_op jit(solution)/shard_map/ppermute | solution.py:316
  19.6 0.0 collective-permute-start.5
  19.6 16.2 %collective-permute-done.3.tall = bf16[1280,256]{1,0:T(8,128)(2,1)S(1)} collective-permute-done((bf16[1280,256]{1,0:T(8,128)(2,1)S(1)}, bf16[1280,256]{1,0:T(8,128)(2,1)S(1)}, u32[]{:S(2)}, u32[]{:S(2)}) %collective-permute-start.3) | collective-permute-done | bytes 655392 | tf_op jit(solution)/shard_map/ppermute | solution.py:321
  35.8 0.0 collective-permute-done.4.wide
  35.8 0.0 copy-done.7
  35.8 0.7 %near_tiles.1 = (f32[64,1024]{1,0:T(8,128)S(1)}, bf16[64,1024]{1,0:T(8,128)(2,1)S(1)}, bf16[64,1024]{1,0:T(8,128)(2,1)S(1)}) custom-call(s32[1,5]{1,0:T(1,128)S(1)} %copy-done.7, bf16[1280,256]{1,0:T(8,128)(2,1)S(1)} %get-tuple-element.41.tall.own_tall, bf16[320,1024]{1,0:T(8,128)(2,1)S(1)} %get-tuple-element.42.wide.own_wide, ...), custom_call_target="tpu_custom_call" | custom-call | flops 1610612736 | bytes 3510292 | tf_op jit(solution)/shard_map/near_tiles/pallas_call | solution.py:300
  36.5 5.6 %collective-permute-start.9 = (bf16[64,1024]{1,0:T(8,128)(2,1)S(1)}, bf16[64,1024]{1,0:T(8,128)(2,1)S(1)}, u32[]{:S(2)}, u32[]{:S(2)}) collective-permute-start(bf16[64,1024]{1,0:T(8,128)(2,1)S(1)} %get-tuple-element.65), channel_id=1, source_target_pairs={{0,28},{2,30},{4,0},{6,2},{8,4},{10,6},{12,8},{14,10},{16,12},{18,... | collective-permute-start | bytes 393224 | tf_op jit(solution)/shard_map/ppermute | solution.py:321
  42.1 0.0 collective-permute-start.10
  42.1 0.0 collective-permute-done.5.refs_0_.first
  42.1 0.0 collective-permute-done.7.refs_2_
  42.1 0.0 collective-permute-done.6.refs_1_
  42.1 0.4 join_round.3
  42.5 0.1 collective-permute-start.8
  42.6 0.0 copy-start.2
  42.6 0.6 %sibling_terms.2 = (f32[64,128]{1,0:T(8,128)S(1)}, f32[64,128]{1,0:T(8,128)S(1)}) custom-call(bf16[256,128]{1,0:T(8,128)(2,1)S(1)} %copy-done.3, bf16[400,128]{1,0:T(8,128)(2,1)S(1)} %collective-permute-done.message.refs_0_.first, bf16[256,128]{1,0:T(8,128)(2,1)S(1)} %get-tuple-element.55.refs_0_, bf16[256,128]{1,0:T(8,128)(2,1)S(1)} %get-tuple-element.56.refs_1_, ...), custom_call_target="tpu_custom_call" | custom-call | flops 33554432 | bytes 397312 | tf_op jit(solution)/shard_map/sibling_terms/pallas_call | solution.py:300
  43.2 0.6 %sibling_terms.3 = (f32[64,128]{1,0:T(8,128)S(1)}, f32[64,128]{1,0:T(8,128)S(1)}) custom-call(bf16[256,128]{1,0:T(8,128)(2,1)S(1)} %get-tuple-element.50.coords, bf16[400,128]{1,0:T(8,128)(2,1)S(1)} %collective-permute-done.5.refs_0_.first, bf16[256,128]{1,0:T(8,128)(2,1)S(1)} %get-tuple-element.60.refs_0_, bf16[256,128]{1,0:T(8,128)(2,1)S(1)} %get-tuple-element.61.refs_1_, ...), custom_call_target="tpu_custom_call" | custom-call | flops 33554432 | bytes 397312 | tf_op jit(solution)/shard_map/sibling_terms/pallas_call | solution.py:300
  43.8 0.1 collective-permute-done.8.refs_0_
  43.8 0.0 copy-done.2
  43.9 1.5 %far_field.1.far = f32[64,1024]{1,0:T(8,128)S(1)} custom-call(bf16[320,128]{1,0:T(8,128)(2,1)S(1)} %get-tuple-element.54.own_top, bf16[4,128,128]{2,1,0:T(8,128)(2,1)S(1)} %bitcast.6, bf16[128,1024]{1,0:T(8,128)(2,1)S(1)} %copy-done.2, bf16[320,128]{1,0:T(8,128)(2,1)S(1)} %collective-permute-done.8.refs_0_, f32[64,128]{1,0:T(8,128)S(1)} %get-tuple-element.58.refs_1_, ...), custom_call_target="tpu_custom_call" | custom-call | flops 33554432 | bytes 950272 | tf_op jit(solution)/shard_map/far_field/pallas_call | solution.py:300
  45.4 0.0 collective-permute-done.9.back
  45.4 1.7 %collective-permute-done.10.side = bf16[64,1024]{1,0:T(8,128)(2,1)S(1)} collective-permute-done((bf16[64,1024]{1,0:T(8,128)(2,1)S(1)}, bf16[64,1024]{1,0:T(8,128)(2,1)S(1)}, u32[]{:S(2)}, u32[]{:S(2)}) %collective-permute-start.10) | collective-permute-done | bytes 131104 | tf_op jit(solution)/shard_map/ppermute | solution.py:316
  47.1 0.8 %total.1 = f32[64,1024]{1,0:T(8,128)} custom-call(f32[64,1024]{1,0:T(8,128)S(1)} %get-tuple-element.45.near, f32[64,1024]{1,0:T(8,128)S(1)} %far_field.1.far, bf16[64,1024]{1,0:T(8,128)(2,1)S(1)} %collective-permute-done.9.back, bf16[64,1024]{1,0:T(8,128)(2,1)S(1)} %collective-permute-done.10.side), custom_call_target="tpu_custom_call" | custom-call | flops 196608 | bytes 1048576 | tf_op jit(solution)/shard_map/total/pallas_call | solution.py:300
Async XLA Ops:
  0.0 7.0 %copy-start = (bf16[256,1024]{1,0:T(8,128)(2,1)S(1)}, bf16[256,1024]{1,0:T(8,128)(2,1)}, u32[]{:S(2)}) copy-start(bf16[256,1024]{1,0:T(8,128)(2,1)} %points.1) | copy-start | bytes 1572868
  3.5 7.2 %collective-permute-start = (bf16[400,128]{1,0:T(8,128)(2,1)}, bf16[400,128]{1,0:T(8,128)(2,1)S(1)}, u32[]{:S(2)}, u32[]{:S(2)}) collective-permute-start(bf16[400,128]{1,0:T(8,128)(2,1)} %get-tuple-element.39), channel_id=1, source_target_pairs={{0,2},{2,0},{4,6},{6,4},{8,10},{10,8},{12,14},{14,12},{16,18},{18,... | collective-permute-start | bytes 307208 | tf_op jit(solution)/shard_map/ppermute | solution.py:316
  5.0 6.6 %collective-permute-start.2 = (bf16[400,128]{1,0:T(8,128)(2,1)}, bf16[400,128]{1,0:T(8,128)(2,1)S(1)}, u32[]{:S(2)}, u32[]{:S(2)}) collective-permute-start(bf16[400,128]{1,0:T(8,128)(2,1)} %get-tuple-element.40), channel_id=1, source_target_pairs={{0,6},{2,4},{4,2},{6,0},{8,14},{10,12},{12,10},{14,8},{16,22},{18,... | collective-permute-start | bytes 307208 | tf_op jit(solution)/shard_map/ppermute | solution.py:316
  6.5 6.3 %collective-permute-start.1 = (bf16[400,128]{1,0:T(8,128)(2,1)}, bf16[400,128]{1,0:T(8,128)(2,1)S(1)}, u32[]{:S(2)}, u32[]{:S(2)}) collective-permute-start(bf16[400,128]{1,0:T(8,128)(2,1)} %get-tuple-element.40), channel_id=1, source_target_pairs={{0,4},{2,6},{4,0},{6,2},{8,12},{10,14},{12,8},{14,10},{16,20},{18,... | collective-permute-start | bytes 307208 | tf_op jit(solution)/shard_map/ppermute | solution.py:316
  7.0 0.9 %copy-start.4 = (bf16[64,1024]{1,0:T(8,128)(2,1)S(1)}, bf16[64,1024]{1,0:T(8,128)(2,1)}, u32[]{:S(2)}) copy-start(bf16[64,1024]{1,0:T(8,128)(2,1)} %get-tuple-element.36.ordered) | copy-start | bytes 393220
  8.1 6.7 %copy-start.1 = (bf16[1,4,128,128]{3,2,1,0:T(8,128)(2,1)S(1)}, bf16[1,4,128,128]{3,2,1,0:T(8,128)(2,1)}, u32[]{:S(2)}) copy-start(bf16[1,4,128,128]{3,2,1,0:T(8,128)(2,1)} %param.13) | copy-start | bytes 393220
  8.1 6.7 %copy-start.3 = (bf16[256,128]{1,0:T(8,128)(2,1)S(1)}, bf16[256,128]{1,0:T(8,128)(2,1)}, u32[]{:S(2)}) copy-start(bf16[256,128]{1,0:T(8,128)(2,1)} %get-tuple-element.46.coords) | copy-start | bytes 196612
  8.2 6.7 %copy-start.5 = (f32[64,128]{1,0:T(8,128)S(1)}, f32[64,128]{1,0:T(8,128)}, u32[]{:S(2)}) copy-start(f32[64,128]{1,0:T(8,128)} %get-tuple-element.47.total) | copy-start | bytes 98308
  10.6 4.3 %copy-start.6 = (s32[1,5,128]{2,0,1:T(1,128)S(1)}, s32[1,5,128]{2,0,1:T(1,128)}, u32[]{:S(2)}) copy-start(s32[1,5,128]{2,0,1:T(1,128)} %param.11) | copy-start | bytes 7684
  12.8 23.0 %collective-permute-start.3 = (bf16[1280,256]{1,0:T(8,128)(2,1)S(1)}, bf16[1280,256]{1,0:T(8,128)(2,1)S(1)}, u32[]{:S(2)}, u32[]{:S(2)}) collective-permute-start(bf16[1280,256]{1,0:T(8,128)(2,1)S(1)} %get-tuple-element.41.tall.own_tall), channel_id=1, source_target_pairs={{0,4},{2,6},{4,8},{6,10},{8,12},{10,14},{12,16},{14,18},{16,20},{1... | collective-permute-start | bytes 1966088 | tf_op jit(solution)/shard_map/ppermute | solution.py:321
  13.5 22.3 %collective-permute-start.4 = (bf16[320,1024]{1,0:T(8,128)(2,1)S(1)}, bf16[320,1024]{1,0:T(8,128)(2,1)S(1)}, u32[]{:S(2)}, u32[]{:S(2)}) collective-permute-start(bf16[320,1024]{1,0:T(8,128)(2,1)S(1)} %get-tuple-element.42.wide.own_wide), channel_id=1, source_target_pairs={{0,2},{2,0},{4,6},{6,4},{8,10},{10,8},{12,14},{14,12},{16,18},{18,... | collective-permute-start | bytes 1966088 | tf_op jit(solution)/shard_map/ppermute | solution.py:316
  15.6 20.2 %copy-start.7 = (s32[1,5]{1,0:T(1,128)S(1)}, s32[1,5]{1,0:T(1,128)}, u32[]{:S(2)}) copy-start(s32[1,5]{1,0:T(1,128)} %mask.1) | copy-start | bytes 64
  15.6 26.5 %collective-permute-start.7 = (bf16[400,128]{1,0:T(8,128)(2,1)S(1)}, bf16[400,128]{1,0:T(8,128)(2,1)S(1)}, u32[]{:S(2)}, u32[]{:S(2)}) collective-permute-start(bf16[400,128]{1,0:T(8,128)(2,1)S(1)} %get-tuple-element.53), channel_id=1, source_target_pairs={{0,24},{2,26},{4,28},{6,30},{8,16},{10,18},{12,20},{14,22},{16,8},... | collective-permute-start | bytes 307208 | tf_op jit(solution)/shard_map/ppermute | solution.py:316
  16.1 26.0 %collective-permute-start.6 = (bf16[400,128]{1,0:T(8,128)(2,1)S(1)}, bf16[400,128]{1,0:T(8,128)(2,1)S(1)}, u32[]{:S(2)}, u32[]{:S(2)}) collective-permute-start(bf16[400,128]{1,0:T(8,128)(2,1)S(1)} %get-tuple-element.53), channel_id=1, source_target_pairs={{0,16},{2,18},{4,20},{6,22},{8,24},{10,26},{12,28},{14,30},{16,0},... | collective-permute-start | bytes 307208 | tf_op jit(solution)/shard_map/ppermute | solution.py:316
  19.6 22.5 %collective-permute-start.5 = (bf16[400,128]{1,0:T(8,128)(2,1)S(1)}, bf16[400,128]{1,0:T(8,128)(2,1)S(1)}, u32[]{:S(2)}, u32[]{:S(2)}) collective-permute-start(bf16[400,128]{1,0:T(8,128)(2,1)S(1)} %get-tuple-element.52), channel_id=1, source_target_pairs={{0,8},{2,10},{4,12},{6,14},{8,0},{10,2},{12,4},{14,6},{16,24},{18,... | collective-permute-start | bytes 307208 | tf_op jit(solution)/shard_map/ppermute | solution.py:316
  36.5 8.9 %collective-permute-start.9 = (bf16[64,1024]{1,0:T(8,128)(2,1)S(1)}, bf16[64,1024]{1,0:T(8,128)(2,1)S(1)}, u32[]{:S(2)}, u32[]{:S(2)}) collective-permute-start(bf16[64,1024]{1,0:T(8,128)(2,1)S(1)} %get-tuple-element.65), channel_id=1, source_target_pairs={{0,28},{2,30},{4,0},{6,2},{8,4},{10,6},{12,8},{14,10},{16,12},{18,... | collective-permute-start | bytes 393224 | tf_op jit(solution)/shard_map/ppermute | solution.py:321
  42.1 5.0 %collective-permute-start.10 = (bf16[64,1024]{1,0:T(8,128)(2,1)S(1)}, bf16[64,1024]{1,0:T(8,128)(2,1)S(1)}, u32[]{:S(2)}, u32[]{:S(2)}) collective-permute-start(bf16[64,1024]{1,0:T(8,128)(2,1)S(1)} %get-tuple-element.66), channel_id=1, source_target_pairs={{0,2},{2,0},{4,6},{6,4},{8,10},{10,8},{12,14},{14,12},{16,18},{18,... | collective-permute-start | bytes 393224 | tf_op jit(solution)/shard_map/ppermute | solution.py:316
  42.5 1.3 %collective-permute-start.8 = (bf16[320,128]{1,0:T(8,128)(2,1)S(1)}, bf16[320,128]{1,0:T(8,128)(2,1)S(1)}, u32[]{:S(2)}, u32[]{:S(2)}) collective-permute-start(bf16[320,128]{1,0:T(8,128)(2,1)S(1)} %get-tuple-element.54.own_top), channel_id=1, source_target_pairs={{0,1},{1,0},{2,3},{3,2},{4,5},{5,4},{6,7},{7,6},{8,9},{9,8},{10,11... | collective-permute-start | bytes 245768 | tf_op jit(solution)/shard_map/ppermute | solution.py:321
  42.6 1.3 %copy-start.2 = (bf16[128,1024]{1,0:T(8,128)(2,1)S(1)}, bf16[128,1024]{1,0:T(8,128)(2,1)}, u32[]{:S(2)}) copy-start(bf16[128,1024]{1,0:T(8,128)(2,1)} %interp.1) | copy-start | bytes 786436
